TPU v7x, 512 devices: a whole 4x8x8 slice. The times are simulated.
512 devices in a mesh: gx: 8 (over y_hi, core), gy: 8 (over y_lo, x), gz: 8 (over z).
Axes of the slice: x: 4, y: 8 (y_hi: 4, y_lo: 2; y = y_hi * 2 + y_lo), z: 8, core: 2. Of those that a mesh axis runs over, the one named last changes fastest.
Arguments:
- populations: float32 [19, 32, 64, 1024], P(None, 'gz', 'gy', 'gx'), as said below
- porosity: float32 [32, 64, 1024], P('gz', 'gy', 'gx'), may hold values from 0 to 1
- node_type: int32 [32, 64, 1024], P('gz', 'gy', 'gx'), may hold values from 0 to 3, as said below
- step_index: int32 [1], replicated, may hold values from 0 to 4095
- adjoint_end: float32 [19, 32, 64, 1024], P(None, 'gz', 'gy', 'gx'), may hold values from -6 to 6
Outputs:
- adjoint_start: float32 [19, 32, 64, 1024], P(None, 'gz', 'gy', 'gx')
- sensitivity: float32 [32, 64, 1024], P('gz', 'gy', 'gx')
Inputs may be any that keep to these rules, and one draw needn't show every extreme that they name: `populations`: every entry is positive, between 0.4 and 1.9 times its velocity's weight. `node_type`: cells of the first and last planes across the span and along the depth are walls, as are scattered obstacle cells; the other cells of the first plane along the stream are inlets, of the last plane outlets.
All inputs are finite; a program needn't handle non-finite values.
Results may differ from a plain program's by a relative error of at most 0.0001.
Values sent between devices are 32-bit elements; how exact they have to be, the bound alone decides.
No kernel may reach another device: no remote copies, remote signals or barrier semaphores. Data moves between devices by JAX's collectives and lax.ppermute only.
A program may use at most 64 MiB of HBM per device.

v0:
```python
import math

import jax
import jax.numpy as jnp
from jax import lax
from jax.sharding import PartitionSpec as P

STEPS = 2


lattice_velocities = (
    (0, 0, 0),
    (1, 0, 0),
    (-1, 0, 0),
    (0, 1, 0),
    (0, -1, 0),
    (0, 0, 1),
    (0, 0, -1),
    (1, 1, 0),
    (-1, -1, 0),
    (1, -1, 0),
    (-1, 1, 0),
    (1, 0, 1),
    (-1, 0, -1),
    (1, 0, -1),
    (-1, 0, 1),
    (0, 1, 1),
    (0, -1, -1),
    (0, 1, -1),
    (0, -1, 1),
)
lattice_weights = (1.0 / 3.0,) + (1.0 / 18.0,) * 6 + (1.0 / 36.0,) * 12
opposite_index = (0, 2, 1, 4, 3, 6, 5, 8, 7, 10, 9, 12, 11, 14, 13, 16, 15, 18, 17)
relax_rate = 1.25
ramp_factor = 0.1
inlet_base = 0.1
inlet_period = 64.0


def with_halo(block, sides, width):
    for axis, dim in sides:
        count = lax.axis_size(axis)
        forward = [(i, i + 1) for i in range(count - 1)]
        forward.append((count - 1, 0))
        backward = [(target, source) for source, target in forward]
        low = lax.ppermute(
            lax.slice_in_dim(block, block.shape[dim] - width, None, axis=dim), axis, forward
        )
        high = lax.ppermute(lax.slice_in_dim(block, 0, width, axis=dim), axis, backward)
        block = jnp.concatenate([low, block, high], axis=dim)
    return block


def lattice_column(which):
    return jnp.asarray([vector[which] for vector in lattice_velocities], jnp.float32)[
        :, None, None, None
    ]


def weight_column():
    return jnp.asarray(lattice_weights, jnp.float32)[:, None, None, None]


def equilibrium(density, flow_east, flow_north, flow_depth):
    projected = (
        lattice_column(0) * flow_east
        + lattice_column(1) * flow_north
        + lattice_column(2) * flow_depth
    )
    square = flow_east * flow_east + flow_north * flow_north + flow_depth * flow_depth
    return (
        weight_column()
        * density
        * (1.0 + 3.0 * projected + 4.5 * projected * projected - 1.5 * square)
    )


def collide(current, porosity, node_kinds, inlet_speed):
    density = jnp.sum(current, axis=0)
    flow_east = jnp.sum(lattice_column(0) * current, axis=0) / density
    flow_north = jnp.sum(lattice_column(1) * current, axis=0) / density
    flow_depth = jnp.sum(lattice_column(2) * current, axis=0) / density
    damping = ramp_factor * (1.0 - porosity) / (ramp_factor + porosity)
    retained = 1.0 - damping
    relaxed = current - relax_rate * (
        current
        - equilibrium(density, retained * flow_east, retained * flow_north, retained * flow_depth)
    )
    bounced = current[jnp.asarray(opposite_index)]
    unit_field = jnp.ones_like(density)
    inflow = equilibrium(unit_field, inlet_speed * unit_field, 0.0 * unit_field, 0.0 * unit_field)
    outflow = equilibrium(density, flow_east, flow_north, flow_depth)
    collided = jnp.where(
        node_kinds == 1,
        bounced,
        jnp.where(node_kinds == 2, inflow, jnp.where(node_kinds == 3, outflow, relaxed)),
    )
    kinetic = flow_east * flow_east + flow_north * flow_north + flow_depth * flow_depth
    energy = jnp.where(node_kinds == 0, damping * density * kinetic, 0.0 * density)
    return (collided, energy)


def inlet_value(step_index, offset):
    moment = (step_index[0] + offset).astype(jnp.float32)
    return inlet_base * (1.0 + 0.8 * jnp.sin(2.0 * math.pi * moment / inlet_period))


def trim_pull(padded, sign):
    extent_z, extent_y, extent_x = padded.shape[1:]
    slabs = []
    for q in range(len(lattice_velocities)):
        vector = lattice_velocities[q]
        move_east = sign * vector[0]
        move_north = sign * vector[1]
        move_depth = sign * vector[2]
        slabs.append(
            padded[
                q,
                1 - move_depth : extent_z - 1 - move_depth,
                1 - move_north : extent_y - 1 - move_north,
                1 - move_east : extent_x - 1 - move_east,
            ]
        )
    return jnp.stack(slabs)


def stream_field(field, sign):
    padded = with_halo(field, (("gx", 3), ("gy", 2), ("gz", 1)), 1)
    return trim_pull(padded, sign)


def on_device(populations, porosity, node_type, step_index, adjoint_end):
    states = []
    current = populations
    for t in range(STEPS):
        states.append(current)
        if t + 1 < STEPS:
            collided, energy = collide(current, porosity, node_type, inlet_value(step_index, t))
            current = stream_field(collided, 1)
    adjoint = adjoint_end
    sensitivity = jnp.zeros_like(porosity)
    for t in reversed(range(STEPS)):
        arriving = stream_field(adjoint, -1)
        inlet_speed = inlet_value(step_index, t)

        def local_step(incoming, design, inlet_speed=inlet_speed):
            return collide(incoming, design, node_type, inlet_speed)

        collided, pullback = jax.vjp(local_step, states[t], porosity)
        adjoint, design_grad = pullback((arriving, jnp.ones_like(porosity)))
        sensitivity = sensitivity + design_grad
    return (adjoint, sensitivity)


def solution(mesh):
    return jax.shard_map(
        on_device,
        mesh=mesh,
        in_specs=(
            P(None, "gz", "gy", "gx"),
            P("gz", "gy", "gx"),
            P("gz", "gy", "gx"),
            P(),
            P(None, "gz", "gy", "gx"),
        ),
        out_specs=(P(None, "gz", "gy", "gx"), P("gz", "gy", "gx")),
        check_vma=False,
    )
```

profile of v0, /device:TPU:40, one launch (start us, length us, event | category | flops | bytes accessed | tf_op | source)
XLA Modules:
  0.0 122.1 jit_solution(7423282609564782685)
XLA Ops:
  6.7 1.9 %collective-permute-start.6 = (f32[19,4,8,1]{3,2,1,0:T(8,128)S(1)}, f32[19,4,8,1]{3,2,1,0:T(8,128)S(1)}, u32[]{:S(2)}, u32[]{:S(2)}) collective-permute-start(f32[19,4,8,1]{3,2,1,0:T(8,128)S(1)} %get-tuple-element.125), channel_id=1, source_target_pairs={{0,64},{64,128},{128,192},{192,256},{256,320},{320,384},{384,448},... | collective-permute-start | bytes 7304 | tf_op jit(solution)/shard_map/ppermute | solution.py:46
  8.6 5.8 %collective-permute-start.7 = (f32[19,4,8,1]{3,2,1,0:T(8,128)S(1)}, f32[19,4,8,1]{3,2,1,0:T(8,128)S(1)}, u32[]{:S(2)}, u32[]{:S(2)}) collective-permute-start(f32[19,4,8,1]{3,2,1,0:T(8,128)S(1)} %get-tuple-element.124), channel_id=1, source_target_pairs={{64,0},{128,64},{192,128},{256,192},{320,256},{384,320},{448,384},... | collective-permute-start | bytes 7304 | tf_op jit(solution)/shard_map/ppermute | solution.py:49
  14.5 1.9 %collective-permute-start = (f32[19,4,8,1]{3,2,1,0:T(8,128)S(1)}, f32[19,4,8,1]{3,2,1,0:T(8,128)S(1)}, u32[]{:S(2)}, u32[]{:S(2)}) collective-permute-start(f32[19,4,8,1]{3,2,1,0:T(8,128)S(1)} %get-tuple-element.127), channel_id=1, source_target_pairs={{64,0},{128,64},{192,128},{256,192},{320,256},{384,320},{448,384},... | collective-permute-start | bytes 7304 | tf_op jit(solution)/shard_map/ppermute | solution.py:49
  16.5 2.4 %collective-permute-start.1 = (f32[19,4,8,1]{3,2,1,0:T(8,128)S(1)}, f32[19,4,8,1]{3,2,1,0:T(8,128)S(1)}, u32[]{:S(2)}, u32[]{:S(2)}) collective-permute-start(f32[19,4,8,1]{3,2,1,0:T(8,128)S(1)} %get-tuple-element.126), channel_id=1, source_target_pairs={{0,64},{64,128},{128,192},{192,256},{256,320},{320,384},{384,448},... | collective-permute-start | bytes 7304 | tf_op jit(solution)/shard_map/ppermute | solution.py:46
  19.5 4.8 %collective-permute-start.8 = (f32[19,4,1,130]{3,2,1,0:T(1,128)S(1)}, f32[19,4,1,130]{3,2,1,0:T(1,128)S(1)}, u32[]{:S(2)}, u32[]{:S(2)}) collective-permute-start(f32[19,4,1,130]{3,2,1,0:T(1,128)S(1)} %get-tuple-element.112), channel_id=1, source_target_pairs={{0,8},{8,16},{16,24},{24,32},{32,40},{40,48},{48,56},{56,0},{1,9},... | collective-permute-start | bytes 118568 | tf_op jit(solution)/shard_map/ppermute | solution.py:46
  24.3 5.9 %collective-permute-start.9 = (f32[19,4,1,130]{3,2,1,0:T(1,128)S(1)}, f32[19,4,1,130]{3,2,1,0:T(1,128)S(1)}, u32[]{:S(2)}, u32[]{:S(2)}) collective-permute-start(f32[19,4,1,130]{3,2,1,0:T(1,128)S(1)} %get-tuple-element.111), channel_id=1, source_target_pairs={{8,0},{16,8},{24,16},{32,24},{40,32},{48,40},{56,48},{0,56},{9,1},... | collective-permute-start | bytes 118568 | tf_op jit(solution)/shard_map/ppermute | solution.py:49
  30.8 5.9 %collective-permute-start.2 = (f32[19,4,1,130]{3,2,1,0:T(1,128)S(1)}, f32[19,4,1,130]{3,2,1,0:T(1,128)S(1)}, u32[]{:S(2)}, u32[]{:S(2)}) collective-permute-start(f32[19,4,1,130]{3,2,1,0:T(1,128)S(1)} %get-tuple-element.114), channel_id=1, source_target_pairs={{8,0},{16,8},{24,16},{32,24},{40,32},{48,40},{56,48},{0,56},{9,1},... | collective-permute-start | bytes 118568 | tf_op jit(solution)/shard_map/ppermute | solution.py:49
  39.3 4.3 %collective-permute-start.10 = (f32[19,1,10,130]{3,2,1,0:T(8,128)S(1)}, f32[19,1,10,130]{3,2,1,0:T(8,128)S(1)}, u32[]{:S(2)}, u32[]{:S(2)}) collective-permute-start(f32[19,1,10,130]{3,2,1,0:T(8,128)S(1)} %get-tuple-element.106), channel_id=1, source_target_pairs={{0,1},{1,2},{2,3},{3,4},{4,5},{5,6},{6,7},{7,0},{8,9},{9,10},{10,1... | collective-permute-start | bytes 296408 | tf_op jit(solution)/shard_map/ppermute | solution.py:46
  43.6 8.6 %collective-permute-start.11 = (f32[19,1,10,130]{3,2,1,0:T(8,128)S(1)}, f32[19,1,10,130]{3,2,1,0:T(8,128)S(1)}, u32[]{:S(2)}, u32[]{:S(2)}) collective-permute-start(f32[19,1,10,130]{3,2,1,0:T(8,128)S(1)} %get-tuple-element.105), channel_id=1, source_target_pairs={{1,0},{2,1},{3,2},{4,3},{5,4},{6,5},{7,6},{0,7},{9,8},{10,9},{11,1... | collective-permute-start | bytes 296408 | tf_op jit(solution)/shard_map/ppermute | solution.py:49
  52.5 3.9 %collective-permute-start.4 = (f32[19,1,10,130]{3,2,1,0:T(8,128)S(1)}, f32[19,1,10,130]{3,2,1,0:T(8,128)S(1)}, u32[]{:S(2)}, u32[]{:S(2)}) collective-permute-start(f32[19,1,10,130]{3,2,1,0:T(8,128)S(1)} %get-tuple-element.108), channel_id=1, source_target_pairs={{1,0},{2,1},{3,2},{4,3},{5,4},{6,5},{7,6},{0,7},{9,8},{10,9},{11,1... | collective-permute-start | bytes 296408 | tf_op jit(solution)/shard_map/ppermute | solution.py:49
  56.4 1.9 %collective-permute-start.5 = (f32[19,1,10,130]{3,2,1,0:T(8,128)S(1)}, f32[19,1,10,130]{3,2,1,0:T(8,128)S(1)}, u32[]{:S(2)}, u32[]{:S(2)}) collective-permute-start(f32[19,1,10,130]{3,2,1,0:T(8,128)S(1)} %get-tuple-element.107), channel_id=1, source_target_pairs={{0,1},{1,2},{2,3},{3,4},{4,5},{5,6},{6,7},{7,0},{8,9},{9,10},{10,1... | collective-permute-start | bytes 296408 | tf_op jit(solution)/shard_map/ppermute | solution.py:46
  61.3 2.3 %collective-permute-done.4 = f32[19,1,10,130]{3,2,1,0:T(8,128)S(1)} collective-permute-done((f32[19,1,10,130]{3,2,1,0:T(8,128)S(1)}, f32[19,1,10,130]{3,2,1,0:T(8,128)S(1)}, u32[]{:S(2)}, u32[]{:S(2)}) %collective-permute-start.4) | collective-permute-done | bytes 98832 | tf_op jit(solution)/shard_map/ppermute | solution.py:49
  63.7 2.8 %collective-permute-done.5 = f32[19,1,10,130]{3,2,1,0:T(8,128)S(1)} collective-permute-done((f32[19,1,10,130]{3,2,1,0:T(8,128)S(1)}, f32[19,1,10,130]{3,2,1,0:T(8,128)S(1)}, u32[]{:S(2)}, u32[]{:S(2)}) %collective-permute-start.5) | collective-permute-done | bytes 98832 | tf_op jit(solution)/shard_map/ppermute | solution.py:46
  71.0 5.3 %collective-permute-start.12 = (f32[19,4,8,1]{3,2,1,0:T(8,128)S(1)}, f32[19,4,8,1]{3,2,1,0:T(8,128)S(1)}, u32[]{:S(2)}, u32[]{:S(2)}) collective-permute-start(f32[19,4,8,1]{3,2,1,0:T(8,128)S(1)} %get-tuple-element.123), channel_id=1, source_target_pairs={{64,0},{128,64},{192,128},{256,192},{320,256},{384,320},{448,384},... | collective-permute-start | bytes 7304 | tf_op jit(solution)/shard_map/ppermute | solution.py:49
  76.3 1.9 %collective-permute-start.13 = (f32[19,4,8,1]{3,2,1,0:T(8,128)S(1)}, f32[19,4,8,1]{3,2,1,0:T(8,128)S(1)}, u32[]{:S(2)}, u32[]{:S(2)}) collective-permute-start(f32[19,4,8,1]{3,2,1,0:T(8,128)S(1)} %get-tuple-element.122), channel_id=1, source_target_pairs={{0,64},{64,128},{128,192},{192,256},{256,320},{320,384},{384,448},... | collective-permute-start | bytes 7304 | tf_op jit(solution)/shard_map/ppermute | solution.py:46
  78.2 5.0 %collective-permute-done.12 = f32[19,4,8,1]{3,2,1,0:T(8,128)S(1)} collective-permute-done((f32[19,4,8,1]{3,2,1,0:T(8,128)S(1)}, f32[19,4,8,1]{3,2,1,0:T(8,128)S(1)}, u32[]{:S(2)}, u32[]{:S(2)}) %collective-permute-start.12) | collective-permute-done | bytes 2464 | tf_op jit(solution)/shard_map/ppermute | solution.py:49
  83.3 6.4 %collective-permute-done.13 = f32[19,4,8,1]{3,2,1,0:T(8,128)S(1)} collective-permute-done((f32[19,4,8,1]{3,2,1,0:T(8,128)S(1)}, f32[19,4,8,1]{3,2,1,0:T(8,128)S(1)}, u32[]{:S(2)}, u32[]{:S(2)}) %collective-permute-start.13) | collective-permute-done | bytes 2464 | tf_op jit(solution)/shard_map/ppermute | solution.py:46
  90.2 4.6 %collective-permute-start.14 = (f32[19,4,1,130]{3,2,1,0:T(1,128)S(1)}, f32[19,4,1,130]{3,2,1,0:T(1,128)S(1)}, u32[]{:S(2)}, u32[]{:S(2)}) collective-permute-start(f32[19,4,1,130]{3,2,1,0:T(1,128)S(1)} %get-tuple-element.110), channel_id=1, source_target_pairs={{8,0},{16,8},{24,16},{32,24},{40,32},{48,40},{56,48},{0,56},{9,1},... | collective-permute-start | bytes 118568 | tf_op jit(solution)/shard_map/ppermute | solution.py:49
  94.8 1.9 %collective-permute-start.15 = (f32[19,4,1,130]{3,2,1,0:T(1,128)S(1)}, f32[19,4,1,130]{3,2,1,0:T(1,128)S(1)}, u32[]{:S(2)}, u32[]{:S(2)}) collective-permute-start(f32[19,4,1,130]{3,2,1,0:T(1,128)S(1)} %get-tuple-element.109), channel_id=1, source_target_pairs={{0,8},{8,16},{16,24},{24,32},{32,40},{40,48},{48,56},{56,0},{1,9},... | collective-permute-start | bytes 118568 | tf_op jit(solution)/shard_map/ppermute | solution.py:46
  96.9 6.3 %collective-permute-done.15 = f32[19,4,1,130]{3,2,1,0:T(1,128)S(1)} collective-permute-done((f32[19,4,1,130]{3,2,1,0:T(1,128)S(1)}, f32[19,4,1,130]{3,2,1,0:T(1,128)S(1)}, u32[]{:S(2)}, u32[]{:S(2)}) %collective-permute-start.15) | collective-permute-done | bytes 39552 | tf_op jit(solution)/shard_map/ppermute | solution.py:46
  103.5 2.9 %collective-permute-start.16 = (f32[19,1,10,130]{3,2,1,0:T(8,128)S(1)}, f32[19,1,10,130]{3,2,1,0:T(8,128)S(1)}, u32[]{:S(2)}, u32[]{:S(2)}) collective-permute-start(f32[19,1,10,130]{3,2,1,0:T(8,128)S(1)} %get-tuple-element.104), channel_id=1, source_target_pairs={{1,0},{2,1},{3,2},{4,3},{5,4},{6,5},{7,6},{0,7},{9,8},{10,9},{11,1... | collective-permute-start | bytes 296408 | tf_op jit(solution)/shard_map/ppermute | solution.py:49
  106.5 2.9 %collective-permute-start.17 = (f32[19,1,10,130]{3,2,1,0:T(8,128)S(1)}, f32[19,1,10,130]{3,2,1,0:T(8,128)S(1)}, u32[]{:S(2)}, u32[]{:S(2)}) collective-permute-start(f32[19,1,10,130]{3,2,1,0:T(8,128)S(1)} %get-tuple-element.103), channel_id=1, source_target_pairs={{0,1},{1,2},{2,3},{3,4},{4,5},{5,6},{6,7},{7,0},{8,9},{9,10},{10,1... | collective-permute-start | bytes 296408 | tf_op jit(solution)/shard_map/ppermute | solution.py:46
  109.5 2.8 %collective-permute-done.16 = f32[19,1,10,130]{3,2,1,0:T(8,128)S(1)} collective-permute-done((f32[19,1,10,130]{3,2,1,0:T(8,128)S(1)}, f32[19,1,10,130]{3,2,1,0:T(8,128)S(1)}, u32[]{:S(2)}, u32[]{:S(2)}) %collective-permute-start.16) | collective-permute-done | bytes 98832 | tf_op jit(solution)/shard_map/ppermute | solution.py:49
  112.4 4.1 %collective-permute-done.17 = f32[19,1,10,130]{3,2,1,0:T(8,128)S(1)} collective-permute-done((f32[19,1,10,130]{3,2,1,0:T(8,128)S(1)}, f32[19,1,10,130]{3,2,1,0:T(8,128)S(1)}, u32[]{:S(2)}, u32[]{:S(2)}) %collective-permute-start.17) | collective-permute-done | bytes 98832 | tf_op jit(solution)/shard_map/ppermute | solution.py:46
  (126 shorter events, 23.6 us)
Async XLA Ops:
  2.8 1.6 %copy-start.1 = (f32[19,4,8,128]{3,2,1,0:T(8,128)S(1)}, f32[19,4,8,128]{3,2,1,0:T(8,128)}, u32[]{:S(2)}) copy-start(f32[19,4,8,128]{3,2,1,0:T(8,128)} %param.45) | copy-start | bytes 933892
  2.8 1.6 %copy-start.5 = (f32[19]{0:T(128)S(1)}, f32[19]{0:T(128)}, u32[]{:S(2)}) copy-start(f32[19]{0:T(128)} %constant.63.clone) | copy-start | bytes 232
  2.8 1.6 %copy-start.6 = (f32[19]{0:T(128)S(1)}, f32[19]{0:T(128)}, u32[]{:S(2)}) copy-start(f32[19]{0:T(128)} %constant.64.clone) | copy-start | bytes 232
  2.8 1.6 %copy-start.7 = (f32[19]{0:T(128)S(1)}, f32[19]{0:T(128)}, u32[]{:S(2)}) copy-start(f32[19]{0:T(128)} %constant.65.clone) | copy-start | bytes 232
  6.5 7.9 %copy-start = (f32[19,4,8,128]{3,2,1,0:T(8,128)S(1)}, f32[19,4,8,128]{3,2,1,0:T(8,128)}, u32[]{:S(2)}) copy-start(f32[19,4,8,128]{3,2,1,0:T(8,128)} %param.49) | copy-start | bytes 933892
  6.7 12.2 %collective-permute-start.6 = (f32[19,4,8,1]{3,2,1,0:T(8,128)S(1)}, f32[19,4,8,1]{3,2,1,0:T(8,128)S(1)}, u32[]{:S(2)}, u32[]{:S(2)}) collective-permute-start(f32[19,4,8,1]{3,2,1,0:T(8,128)S(1)} %get-tuple-element.125), channel_id=1, source_target_pairs={{0,64},{64,128},{128,192},{192,256},{256,320},{320,384},{384,448},... | collective-permute-start | bytes 7304 | tf_op jit(solution)/shard_map/ppermute | solution.py:46
  8.6 10.3 %collective-permute-start.7 = (f32[19,4,8,1]{3,2,1,0:T(8,128)S(1)}, f32[19,4,8,1]{3,2,1,0:T(8,128)S(1)}, u32[]{:S(2)}, u32[]{:S(2)}) collective-permute-start(f32[19,4,8,1]{3,2,1,0:T(8,128)S(1)} %get-tuple-element.124), channel_id=1, source_target_pairs={{64,0},{128,64},{192,128},{256,192},{320,256},{384,320},{448,384},... | collective-permute-start | bytes 7304 | tf_op jit(solution)/shard_map/ppermute | solution.py:49
  14.5 15.7 %collective-permute-start = (f32[19,4,8,1]{3,2,1,0:T(8,128)S(1)}, f32[19,4,8,1]{3,2,1,0:T(8,128)S(1)}, u32[]{:S(2)}, u32[]{:S(2)}) collective-permute-start(f32[19,4,8,1]{3,2,1,0:T(8,128)S(1)} %get-tuple-element.127), channel_id=1, source_target_pairs={{64,0},{128,64},{192,128},{256,192},{320,256},{384,320},{448,384},... | collective-permute-start | bytes 7304 | tf_op jit(solution)/shard_map/ppermute | solution.py:49
  16.5 13.8 %collective-permute-start.1 = (f32[19,4,8,1]{3,2,1,0:T(8,128)S(1)}, f32[19,4,8,1]{3,2,1,0:T(8,128)S(1)}, u32[]{:S(2)}, u32[]{:S(2)}) collective-permute-start(f32[19,4,8,1]{3,2,1,0:T(8,128)S(1)} %get-tuple-element.126), channel_id=1, source_target_pairs={{0,64},{64,128},{128,192},{192,256},{256,320},{320,384},{384,448},... | collective-permute-start | bytes 7304 | tf_op jit(solution)/shard_map/ppermute | solution.py:46
  19.5 19.4 %collective-permute-start.8 = (f32[19,4,1,130]{3,2,1,0:T(1,128)S(1)}, f32[19,4,1,130]{3,2,1,0:T(1,128)S(1)}, u32[]{:S(2)}, u32[]{:S(2)}) collective-permute-start(f32[19,4,1,130]{3,2,1,0:T(1,128)S(1)} %get-tuple-element.112), channel_id=1, source_target_pairs={{0,8},{8,16},{16,24},{24,32},{32,40},{40,48},{48,56},{56,0},{1,9},... | collective-permute-start | bytes 118568 | tf_op jit(solution)/shard_map/ppermute | solution.py:46
  24.3 14.6 %collective-permute-start.9 = (f32[19,4,1,130]{3,2,1,0:T(1,128)S(1)}, f32[19,4,1,130]{3,2,1,0:T(1,128)S(1)}, u32[]{:S(2)}, u32[]{:S(2)}) collective-permute-start(f32[19,4,1,130]{3,2,1,0:T(1,128)S(1)} %get-tuple-element.111), channel_id=1, source_target_pairs={{8,0},{16,8},{24,16},{32,24},{40,32},{48,40},{56,48},{0,56},{9,1},... | collective-permute-start | bytes 118568 | tf_op jit(solution)/shard_map/ppermute | solution.py:49
  30.8 21.4 %collective-permute-start.2 = (f32[19,4,1,130]{3,2,1,0:T(1,128)S(1)}, f32[19,4,1,130]{3,2,1,0:T(1,128)S(1)}, u32[]{:S(2)}, u32[]{:S(2)}) collective-permute-start(f32[19,4,1,130]{3,2,1,0:T(1,128)S(1)} %get-tuple-element.114), channel_id=1, source_target_pairs={{8,0},{16,8},{24,16},{32,24},{40,32},{48,40},{56,48},{0,56},{9,1},... | collective-permute-start | bytes 118568 | tf_op jit(solution)/shard_map/ppermute | solution.py:49
  36.7 15.5 %collective-permute-start.3 = (f32[19,4,1,130]{3,2,1,0:T(1,128)S(1)}, f32[19,4,1,130]{3,2,1,0:T(1,128)S(1)}, u32[]{:S(2)}, u32[]{:S(2)}) collective-permute-start(f32[19,4,1,130]{3,2,1,0:T(1,128)S(1)} %get-tuple-element.113), channel_id=1, source_target_pairs={{0,8},{8,16},{16,24},{24,32},{32,40},{40,48},{48,56},{56,0},{1,9},... | collective-permute-start | bytes 118568 | tf_op jit(solution)/shard_map/ppermute | solution.py:46
  39.3 19.4 %collective-permute-start.10 = (f32[19,1,10,130]{3,2,1,0:T(8,128)S(1)}, f32[19,1,10,130]{3,2,1,0:T(8,128)S(1)}, u32[]{:S(2)}, u32[]{:S(2)}) collective-permute-start(f32[19,1,10,130]{3,2,1,0:T(8,128)S(1)} %get-tuple-element.106), channel_id=1, source_target_pairs={{0,1},{1,2},{2,3},{3,4},{4,5},{5,6},{6,7},{7,0},{8,9},{9,10},{10,1... | collective-permute-start | bytes 296408 | tf_op jit(solution)/shard_map/ppermute | solution.py:46
  43.6 16.4 %collective-permute-start.11 = (f32[19,1,10,130]{3,2,1,0:T(8,128)S(1)}, f32[19,1,10,130]{3,2,1,0:T(8,128)S(1)}, u32[]{:S(2)}, u32[]{:S(2)}) collective-permute-start(f32[19,1,10,130]{3,2,1,0:T(8,128)S(1)} %get-tuple-element.105), channel_id=1, source_target_pairs={{1,0},{2,1},{3,2},{4,3},{5,4},{6,5},{7,6},{0,7},{9,8},{10,9},{11,1... | collective-permute-start | bytes 296408 | tf_op jit(solution)/shard_map/ppermute | solution.py:49
  52.5 11.1 %collective-permute-start.4 = (f32[19,1,10,130]{3,2,1,0:T(8,128)S(1)}, f32[19,1,10,130]{3,2,1,0:T(8,128)S(1)}, u32[]{:S(2)}, u32[]{:S(2)}) collective-permute-start(f32[19,1,10,130]{3,2,1,0:T(8,128)S(1)} %get-tuple-element.108), channel_id=1, source_target_pairs={{1,0},{2,1},{3,2},{4,3},{5,4},{6,5},{7,6},{0,7},{9,8},{10,9},{11,1... | collective-permute-start | bytes 296408 | tf_op jit(solution)/shard_map/ppermute | solution.py:49
  56.4 10.0 %collective-permute-start.5 = (f32[19,1,10,130]{3,2,1,0:T(8,128)S(1)}, f32[19,1,10,130]{3,2,1,0:T(8,128)S(1)}, u32[]{:S(2)}, u32[]{:S(2)}) collective-permute-start(f32[19,1,10,130]{3,2,1,0:T(8,128)S(1)} %get-tuple-element.107), channel_id=1, source_target_pairs={{0,1},{1,2},{2,3},{3,4},{4,5},{5,6},{6,7},{7,0},{8,9},{9,10},{10,1... | collective-permute-start | bytes 296408 | tf_op jit(solution)/shard_map/ppermute | solution.py:46
  71.0 12.3 %collective-permute-start.12 = (f32[19,4,8,1]{3,2,1,0:T(8,128)S(1)}, f32[19,4,8,1]{3,2,1,0:T(8,128)S(1)}, u32[]{:S(2)}, u32[]{:S(2)}) collective-permute-start(f32[19,4,8,1]{3,2,1,0:T(8,128)S(1)} %get-tuple-element.123), channel_id=1, source_target_pairs={{64,0},{128,64},{192,128},{256,192},{320,256},{384,320},{448,384},... | collective-permute-start | bytes 7304 | tf_op jit(solution)/shard_map/ppermute | solution.py:49
  76.3 13.4 %collective-permute-start.13 = (f32[19,4,8,1]{3,2,1,0:T(8,128)S(1)}, f32[19,4,8,1]{3,2,1,0:T(8,128)S(1)}, u32[]{:S(2)}, u32[]{:S(2)}) collective-permute-start(f32[19,4,8,1]{3,2,1,0:T(8,128)S(1)} %get-tuple-element.122), channel_id=1, source_target_pairs={{0,64},{64,128},{128,192},{192,256},{256,320},{320,384},{384,448},... | collective-permute-start | bytes 7304 | tf_op jit(solution)/shard_map/ppermute | solution.py:46
  90.2 6.6 %collective-permute-start.14 = (f32[19,4,1,130]{3,2,1,0:T(1,128)S(1)}, f32[19,4,1,130]{3,2,1,0:T(1,128)S(1)}, u32[]{:S(2)}, u32[]{:S(2)}) collective-permute-start(f32[19,4,1,130]{3,2,1,0:T(1,128)S(1)} %get-tuple-element.110), channel_id=1, source_target_pairs={{8,0},{16,8},{24,16},{32,24},{40,32},{48,40},{56,48},{0,56},{9,1},... | collective-permute-start | bytes 118568 | tf_op jit(solution)/shard_map/ppermute | solution.py:49
  94.8 8.4 %collective-permute-start.15 = (f32[19,4,1,130]{3,2,1,0:T(1,128)S(1)}, f32[19,4,1,130]{3,2,1,0:T(1,128)S(1)}, u32[]{:S(2)}, u32[]{:S(2)}) collective-permute-start(f32[19,4,1,130]{3,2,1,0:T(1,128)S(1)} %get-tuple-element.109), channel_id=1, source_target_pairs={{0,8},{8,16},{16,24},{24,32},{32,40},{40,48},{48,56},{56,0},{1,9},... | collective-permute-start | bytes 118568 | tf_op jit(solution)/shard_map/ppermute | solution.py:46
  103.5 8.8 %collective-permute-start.16 = (f32[19,1,10,130]{3,2,1,0:T(8,128)S(1)}, f32[19,1,10,130]{3,2,1,0:T(8,128)S(1)}, u32[]{:S(2)}, u32[]{:S(2)}) collective-permute-start(f32[19,1,10,130]{3,2,1,0:T(8,128)S(1)} %get-tuple-element.104), channel_id=1, source_target_pairs={{1,0},{2,1},{3,2},{4,3},{5,4},{6,5},{7,6},{0,7},{9,8},{10,9},{11,1... | collective-permute-start | bytes 296408 | tf_op jit(solution)/shard_map/ppermute | solution.py:49
  106.5 10.0 %collective-permute-start.17 = (f32[19,1,10,130]{3,2,1,0:T(8,128)S(1)}, f32[19,1,10,130]{3,2,1,0:T(8,128)S(1)}, u32[]{:S(2)}, u32[]{:S(2)}) collective-permute-start(f32[19,1,10,130]{3,2,1,0:T(8,128)S(1)} %get-tuple-element.103), channel_id=1, source_target_pairs={{0,1},{1,2},{2,3},{3,4},{4,5},{5,6},{6,7},{7,0},{8,9},{9,10},{10,1... | collective-permute-start | bytes 296408 | tf_op jit(solution)/shard_map/ppermute | solution.py:46
  121.4 0.7 copy-start.2
  (5 other events, 3.4 us)
where the time goes:
time: 123 us; the launch traced here: 122 us
  starting transfers between devices  68.8 us (56%)
  waiting for transfers between devices  30.9 us (25%)
  other arithmetic  15.6 us (13%)
  local copies, waits for them, and re-layouts  4.86 us (4%)
  between operations  1.9 us (2%)
    ppermute x9, starting transfers between devices, with_halo(): lax.ppermute(lax.slice_in_dim(block, 0, width, axis=dim), axis, backward)  44.8 us
    ppermute x9, starting transfers between devices, with_halo(): lax.ppermute(lax.slice_in_dim(block, block.shape[dim] - width, None, axis...  24 us
    ppermute x9, waiting for transfers between devices, with_halo(): lax.ppermute(lax.slice_in_dim(block, block.shape[dim] - width, None, axis...  19.6 us
    ppermute x9, waiting for transfers between devices, with_halo(): lax.ppermute(lax.slice_in_dim(block, 0, width, axis=dim), axis, backward)  11.3 us
    unnamed x51, other arithmetic  4.06 us
    scatter-add x2, other arithmetic, collide(): bounced = current[jnp.asarray(opposite_index)]  3.81 us
    unnamed x25, local copies, waits for them, and re-layouts  2.83 us
    concatenate x6, other arithmetic, with_halo(): block = jnp.concatenate([low, block, high], axis=dim)  2.6 us
  transfers between devices with their start and end apart: 18, of which 8 were waited for; matrix products, arithmetic and copies ran while one was open for 4% of the time, Pallas kernels for 0%

commit v1 on v0

v1 whole, which is shorter than its diff:
```python
import math

import jax
import jax.numpy as jnp
from jax import lax
from jax.sharding import PartitionSpec as P

VELOCITIES = (
    (0, 0, 0),
    (1, 0, 0),
    (-1, 0, 0),
    (0, 1, 0),
    (0, -1, 0),
    (0, 0, 1),
    (0, 0, -1),
    (1, 1, 0),
    (-1, -1, 0),
    (1, -1, 0),
    (-1, 1, 0),
    (1, 0, 1),
    (-1, 0, -1),
    (1, 0, -1),
    (-1, 0, 1),
    (0, 1, 1),
    (0, -1, -1),
    (0, 1, -1),
    (0, -1, 1),
)
WEIGHTS = (1.0 / 3.0,) + (1.0 / 18.0,) * 6 + (1.0 / 36.0,) * 12
OPPOSITE = (0, 2, 1, 4, 3, 6, 5, 8, 7, 10, 9, 12, 11, 14, 13, 16, 15, 18, 17)
Q = 19
RATE = 1.25
RAMP = 0.1


def add_up(terms):
    total = None
    for sign, value in terms:
        if total is None:
            total = value if sign > 0 else -value
        else:
            total = total + value if sign > 0 else total - value
    return total


def moments(f):
    density = add_up([(1, f[q]) for q in range(Q)])
    flow = [
        add_up([(VELOCITIES[q][i], f[q]) for q in range(Q) if VELOCITIES[q][i]])
        for i in range(3)
    ]
    return density, flow


def along(q, vector):
    return add_up([(VELOCITIES[q][i], vector[i]) for i in range(3) if VELOCITIES[q][i]])


def damping_of(porosity):
    return RAMP * (1.0 - porosity) / (RAMP + porosity)


def collide(f, porosity, kinds, speed):
    density, flow = moments(f)
    inverse = 1.0 / density
    kept = jnp.where(kinds == 0, 1.0 - damping_of(porosity), 1.0)
    inlet = kinds == 2
    v = [jnp.where(inlet, speed if i == 0 else 0.0, flow[i] * inverse * kept) for i in range(3)]
    r = jnp.where(inlet, 1.0, density)
    fluid = kinds == 0
    wall = kinds == 1
    scale = jnp.where(fluid, RATE, 1.0) * r
    keep = jnp.where(fluid, 1.0 - RATE, 0.0)
    base = 1.0 - 1.5 * (v[0] * v[0] + v[1] * v[1] + v[2] * v[2])
    out = []
    for q in range(Q):
        p = along(q, v)
        shape = base if p is None else base + p * (3.0 + 4.5 * p)
        out.append(jnp.where(wall, f[OPPOSITE[q]], keep * f[q] + (WEIGHTS[q] * scale) * shape))
    return out


def pull_back(density, flow, h, porosity, kinds):
    fluid = kinds == 0
    wall = kinds == 1
    outlet = kinds == 3
    inverse = 1.0 / density
    u = [flow[i] * inverse for i in range(3)]
    square = u[0] * u[0] + u[1] * u[1] + u[2] * u[2]
    ramp = 1.0 / (RAMP + porosity)
    damping = jnp.where(fluid, RAMP * (1.0 - porosity) * ramp, 0.0)
    kept = 1.0 - damping
    v = [kept * u[i] for i in range(3)]
    wh = [WEIGHTS[q] * h[q] for q in range(Q)]
    zero, first = moments(wh)
    second = {}
    for i in range(3):
        for j in range(i, 3):
            second[i, j] = second[j, i] = add_up(
                [
                    (VELOCITIES[q][i] * VELOCITIES[q][j], wh[q])
                    for q in range(Q)
                    if VELOCITIES[q][i] * VELOCITIES[q][j]
                ]
            )
    bent = [
        4.5 * (second[i, 0] * v[0] + second[i, 1] * v[1] + second[i, 2] * v[2]) - 1.5 * zero * v[i]
        for i in range(3)
    ]
    slope = [3.0 * first[i] + 2.0 * bent[i] for i in range(3)]
    level = zero + sum(v[i] * (3.0 * first[i] + bent[i]) for i in range(3))
    rate = jnp.where(fluid, RATE, jnp.where(outlet, 1.0, 0.0))
    keep = jnp.where(fluid, 1.0 - RATE, 0.0)
    turn = sum(slope[i] * u[i] for i in range(3))
    tilt = [rate * kept * slope[i] + 2.0 * damping * u[i] for i in range(3)]
    flat = rate * (level - kept * turn) - damping * square
    out = []
    for q in range(Q):
        p = along(q, tilt)
        moved = keep * h[q] + (flat if p is None else flat + p)
        out.append(jnp.where(wall, h[OPPOSITE[q]], moved))
    by_porosity = jnp.where(
        fluid,
        (-RAMP * (1.0 + RAMP)) * ramp * ramp * density * (square - RATE * turn),
        0.0,
    )
    return out, by_porosity


def with_halo(block, axis, dim, width):
    count = lax.axis_size(axis)
    forward = [(i, (i + 1) % count) for i in range(count)]
    backward = [(t, s) for s, t in forward]
    low = lax.ppermute(
        lax.slice_in_dim(block, block.shape[dim] - width, None, axis=dim), axis, forward
    )
    high = lax.ppermute(lax.slice_in_dim(block, 0, width, axis=dim), axis, backward)
    return jnp.concatenate([low, block, high], axis=dim)


def shifted(field, shift):
    return field[
        tuple(slice(1 - s, field.shape[i] - 1 - s) for i, s in enumerate(reversed(shift)))
    ]


def inner(field):
    return field[1:-1, 1:-1, 1:-1]


def on_device(populations, porosity, node_type, step_index, adjoint_end):
    moment = step_index[0].astype(jnp.float32)
    speed = 0.1 * (1.0 + 0.8 * jnp.sin(2.0 * math.pi * moment / 64.0))
    f = [populations[q] for q in range(Q)]
    collided = collide(f, porosity, node_type, speed)
    whole = jnp.concatenate(
        [
            jnp.stack(collided),
            adjoint_end,
            porosity[None],
            node_type.astype(jnp.float32)[None],
        ]
    )
    for axis, dim in (("gz", 1), ("gy", 2), ("gx", 3)):
        whole = with_halo(whole, axis, dim, 2)
    later = [shifted(whole[q], VELOCITIES[q]) for q in range(Q)]
    h = [shifted(whole[Q + q], tuple(-c for c in VELOCITIES[q])) for q in range(Q)]
    design, kinds = inner(whole[2 * Q]), inner(whole[2 * Q + 1])
    density, flow = moments(later)
    adjoint, sense = pull_back(density, flow, h, design, kinds)
    h = [shifted(adjoint[q], tuple(-c for c in VELOCITIES[q])) for q in range(Q)]
    density, flow = moments(f)
    adjoint, by_porosity = pull_back(density, flow, h, porosity, node_type)
    return jnp.stack(adjoint), inner(sense) + by_porosity


def solution(mesh):
    brick = P(None, "gz", "gy", "gx")
    field = P("gz", "gy", "gx")
    return jax.shard_map(
        on_device,
        mesh=mesh,
        in_specs=(brick, field, field, P(), brick),
        out_specs=(brick, field),
        check_vma=False,
    )
```

time: 123 us -> 79.4 us (0.65)
  the two profiles are of different devices: /device:TPU:40 before, /device:TPU:23 now
where the time goes in v1:
time: 79.4 us; the launch traced here: 78.7 us
  starting transfers between devices  27.1 us (34%)
  waiting for transfers between devices  21.2 us (27%)
  local copies, waits for them, and re-layouts  16.8 us (21%)
  other arithmetic  11.9 us (15%)
  between operations  1.77 us (2%)
    ppermute x3, starting transfers between devices, with_halo(): lax.ppermute(lax.slice_in_dim(block, block.shape[dim] - width, None, axis...  14.3 us
    ppermute x3, starting transfers between devices, with_halo(): lax.ppermute(lax.slice_in_dim(block, 0, width, axis=dim), axis, backward)  12.8 us
    ppermute x3, waiting for transfers between devices, with_halo(): lax.ppermute(lax.slice_in_dim(block, 0, width, axis=dim), axis, backward)  11.4 us
    ppermute x3, waiting for transfers between devices, with_halo(): lax.ppermute(lax.slice_in_dim(block, block.shape[dim] - width, None, axis...  9.75 us
    concatenate x2, other arithmetic, with_halo(): return jnp.concatenate([low, block, high], axis=dim)  5.7 us
    slice x3, local copies, waits for them, and re-layouts, with_halo(): lax.slice_in_dim(block, block.shape[dim] - width, None, axis=dim)  4.76 us
    ppermute x1, local copies, waits for them, and re-layouts, with_halo(): lax.ppermute(lax.slice_in_dim(block, 0, width, axis=dim), axis, backward)  3.68 us
    unnamed x37, other arithmetic  2.8 us
  transfers between devices with their start and end apart: 6, of which 5 were waited for; matrix products, arithmetic and copies ran while one was open for 4% of the time, Pallas kernels for 0%

profile of v1, /device:TPU:23, one launch (start us, length us, event | category | flops | bytes accessed | tf_op | source)
XLA Modules:
  0.0 78.7 jit_solution(755070001411104936)
XLA Ops:
  1.4 0.7 convert_bitcast_fusion
  2.1 0.9 %fusion.171 = (f32[1,4,8,128]{3,2,1,0:T(8,128)S(1)}, f32[1,4,8,128]{3,2,1,0:T(8,128)S(1)}, f32[1,4,8,128]{3,2,1,0:T(8,128)S(1)}, f32[1,4,8,128]{3,2,1,0:T(8,128)...) fusion(f32[19,4,8,128]{3,2,1,0:T(8,128)} %param.5), kind=kLoop, calls=%fused_computation.464 | loop fusion | bytes 622592 | tf_op jit(solution)/shard_map/slice | solution.py:154
  3.1 1.5 %constant_dynamic-update-slice_fusion.20 = (f32[40,4,8,128]{3,1,2,0:T(4,128)S(1)}, f32[4,8,128]{2,0,1:T(4,128)S(1)}, f32[4,8,128]{2,0,1:T(4,128)S(1)}, f32[4,8,1...) fusion(f32[1,4,8,128]{3,2,1,0:T(8,128)S(1)} %get-tuple-element., ...), kind=kLoop, calls=%fused_computation.104 | loop fusion | flops 327679 | bytes 516100
  5.7 4.0 %collective-permute-start = (f32[40,2,8,128]{3,1,2,0:T(2,128)S(1)}, f32[40,2,8,128]{3,1,2,0:T(2,128)S(1)}, u32[]{:S(2)}, u32[]{:S(2)}) collective-permute-start(f32[40,2,8,128]{3,1,2,0:T(2,128)S(1)} %get-tuple-element.121), channel_id=1, source_target_pairs={{0,1},{1,2},{2,3},{3,4},{4,5},{5,6},{6,7},{7,0},{8,9},{9,10},{10,1... | collective-permute-start | bytes 983048 | tf_op jit(solution)/shard_map/ppermute | solution.py:134
  9.7 8.6 %collective-permute-start.1 = (f32[40,2,8,128]{3,1,2,0:T(2,128)S(1)}, f32[40,2,8,128]{3,1,2,0:T(2,128)S(1)}, u32[]{:S(2)}, u32[]{:S(2)}) collective-permute-start(f32[40,2,8,128]{3,1,2,0:T(2,128)S(1)} %get-tuple-element.122), channel_id=1, source_target_pairs={{1,0},{2,1},{3,2},{4,3},{5,4},{6,5},{7,6},{0,7},{9,8},{10,9},{11,1... | collective-permute-start | bytes 983048 | tf_op jit(solution)/shard_map/ppermute | solution.py:137
  18.3 5.5 %collective-permute-done = f32[40,2,8,128]{3,1,2,0:T(2,128)S(1)} collective-permute-done((f32[40,2,8,128]{3,1,2,0:T(2,128)S(1)}, f32[40,2,8,128]{3,1,2,0:T(2,128)S(1)}, u32[]{:S(2)}, u32[]{:S(2)}) %collective-permute-start) | collective-permute-done | bytes 327712 | tf_op jit(solution)/shard_map/ppermute | solution.py:134
  23.8 0.9 %collective-permute-done.1 = f32[40,2,8,128]{3,1,2,0:T(2,128)S(1)} collective-permute-done((f32[40,2,8,128]{3,1,2,0:T(2,128)S(1)}, f32[40,2,8,128]{3,1,2,0:T(2,128)S(1)}, u32[]{:S(2)}, u32[]{:S(2)}) %collective-permute-start.1) | collective-permute-done | bytes 327712 | tf_op jit(solution)/shard_map/ppermute | solution.py:137
  24.8 3.1 %collective-permute-start.2 = (f32[40,8,2,128]{3,1,2,0:T(8,128)S(1)}, f32[40,8,2,128]{3,1,2,0:T(8,128)S(1)}, u32[]{:S(2)}, u32[]{:S(2)}) collective-permute-start(f32[40,8,2,128]{3,1,2,0:T(8,128)S(1)} %get-tuple-element.119), channel_id=1, source_target_pairs={{0,8},{8,16},{16,24},{24,32},{32,40},{40,48},{48,56},{56,0},{1,9},... | collective-permute-start | bytes 983048 | tf_op jit(solution)/shard_map/ppermute | solution.py:134
  28.0 2.2 %collective-permute-start.3 = (f32[40,8,2,128]{3,1,2,0:T(8,128)S(1)}, f32[40,8,2,128]{3,1,2,0:T(8,128)S(1)}, u32[]{:S(2)}, u32[]{:S(2)}) collective-permute-start(f32[40,8,2,128]{3,1,2,0:T(8,128)S(1)} %get-tuple-element.120), channel_id=1, source_target_pairs={{8,0},{16,8},{24,16},{32,24},{40,32},{48,40},{56,48},{0,56},{9,1},... | collective-permute-start | bytes 983048 | tf_op jit(solution)/shard_map/ppermute | solution.py:137
  30.1 4.3 %collective-permute-done.2 = f32[40,8,2,128]{3,1,2,0:T(8,128)S(1)} collective-permute-done((f32[40,8,2,128]{3,1,2,0:T(8,128)S(1)}, f32[40,8,2,128]{3,1,2,0:T(8,128)S(1)}, u32[]{:S(2)}, u32[]{:S(2)}) %collective-permute-start.2) | collective-permute-done | bytes 327712 | tf_op jit(solution)/shard_map/ppermute | solution.py:134
  34.4 5.0 %collective-permute-done.3 = f32[40,8,2,128]{3,1,2,0:T(8,128)S(1)} collective-permute-done((f32[40,8,2,128]{3,1,2,0:T(8,128)S(1)}, f32[40,8,2,128]{3,1,2,0:T(8,128)S(1)}, u32[]{:S(2)}, u32[]{:S(2)}) %collective-permute-start.3) | collective-permute-done | bytes 327712 | tf_op jit(solution)/shard_map/ppermute | solution.py:137
  39.4 0.7 copy-done.1
  40.6 2.0 %fusion.169 = (f32[40,8,12,2]{3,1,2,0:T(8,128)}, f32[40,8,12,2]{3,1,2,0:T(8,128)S(1)}) fusion(f32[40,8,12,128]{3,1,2,0:T(8,128)S(1)} %pad_maximum_fusion.1), kind=kLoop, calls=%fused_computation.462 | loop fusion | bytes 122880 | tf_op jit(solution)/shard_map/slice | solution.py:135
  42.6 2.5 %copy.137 = f32[40,8,12,2]{0,1,3,2:T(8,128)S(1)} copy(f32[40,8,12,2]{3,1,2,0:T(8,128)} %get-tuple-element.117) | data formatting | bytes 61440 | tf_op jit(solution)/shard_map/slice | solution.py:135
  45.1 7.2 %collective-permute-start.4 = (f32[40,8,12,2]{0,1,3,2:T(8,128)S(1)}, f32[40,8,12,2]{0,1,3,2:T(8,128)S(1)}, u32[]{:S(2)}, u32[]{:S(2)}) collective-permute-start(f32[40,8,12,2]{0,1,3,2:T(8,128)S(1)} %copy.137), channel_id=1, source_target_pairs={{0,64},{64,128},{128,192},{192,256},{256,320},{320,384},{384,448},... | collective-permute-start | bytes 92168 | tf_op jit(solution)/shard_map/ppermute | solution.py:134
  52.2 1.7 %copy.138 = f32[40,8,12,2]{0,1,3,2:T(8,128)} copy(f32[40,8,12,2]{3,1,2,0:T(8,128)S(1)} %get-tuple-element.118) | data formatting | bytes 61440 | tf_op jit(solution)/shard_map/slice | solution.py:137
  53.9 2.1 %collective-permute-start.5 = (f32[40,8,12,2]{0,1,3,2:T(8,128)}, f32[40,8,12,2]{0,1,3,2:T(8,128)}, u32[]{:S(2)}, u32[]{:S(2)}) collective-permute-start(f32[40,8,12,2]{0,1,3,2:T(8,128)} %copy.138), channel_id=1, source_target_pairs={{64,0},{128,64},{192,128},{256,192},{320,256},{384,320},{448,384},... | collective-permute-start | bytes 92168 | tf_op jit(solution)/shard_map/ppermute | solution.py:137
  56.0 1.7 %copy.139 = f32[40,8,12,2]{3,1,2,0:T(8,128)S(1)} copy(f32[40,8,12,2]{0,1,3,2:T(8,128)S(1)} %collective-permute-done.4) | data formatting | bytes 61440 | tf_op jit(solution)/shard_map/ppermute | solution.py:134
  57.7 5.6 %collective-permute-done.5 = f32[40,8,12,2]{0,1,3,2:T(8,128)} collective-permute-done((f32[40,8,12,2]{0,1,3,2:T(8,128)}, f32[40,8,12,2]{0,1,3,2:T(8,128)}, u32[]{:S(2)}, u32[]{:S(2)}) %collective-permute-start.5) | collective-permute-done | bytes 30752 | tf_op jit(solution)/shard_map/ppermute | solution.py:137
  63.3 3.7 %copy.140 = f32[40,8,12,2]{3,1,2,0:T(8,128)} copy(f32[40,8,12,2]{0,1,3,2:T(8,128)} %collective-permute-done.5) | data formatting | bytes 61440 | tf_op jit(solution)/shard_map/ppermute | solution.py:137
  67.0 5.2 %pad_maximum_fusion = f32[40,8,12,132]{3,1,2,0:T(8,128)S(1)} fusion(f32[40,8,12,2]{3,1,2,0:T(8,128)} %copy.140, f32[40,8,2,128]{3,1,2,0:T(8,128)} %copy-done.1, f32[40,2,8,128]{3,1,2,0:T(2,128)S(1)} %collective-permute-done.1, f32[40,4,8,128]{3,1,2,0:T(4,128)S(1)} %constant_dynamic-update-slice_fusion, f32[40,2,8,128]{3,1,2,0:T(2,128)S(1)} %collective-permute-done, ...), kind=kLoop, calls=%fused_computation | loop fusion | flops 3041280 | bytes 4055040 | tf_op jit(solution)/shard_map/concatenate | solution.py:138
  74.0 1.0 %multiply_add_fusion.4 = (f32[6,10,130]{2,0,1:T(8,128)S(1)}, f32[6,10,130]{2,0,1:T(8,128)S(1)}, f32[6,10,130]{2,0,1:T(8,128)S(1)}, f32[6,10,130]{2,0,1:T(8,128)S...) fusion(f32[8,12,132]{2,0,1:T(8,128)S(1)} %get-tuple-element.97,, ...), kind=kLoop, calls=%fused_computation.147 | loop fusion | flops 1552200 | bytes 1723800 | tf_op jit(solution)/shard_map/add | solution.py:114
  75.7 0.9 %fusion.24 = (f32[4,8,128]{2,0,1:T(4,128)S(1)}, f32[4,8,128]{2,0,1:T(4,128)S(1)}, f32[4,8,128]{2,0,1:T(4,128)S(1)}, f32[4,8,128]{2,0,1:T(4,128)S(1)}, f32[4,8,12...) fusion(pred[4,8,128]{2,0,1:T(4,128)(4,1)S(1)} %get-tuple-elemen, ...), kind=kLoop, calls=%fused_computation.187 | loop fusion | flops 1052672 | bytes 2396160 | tf_op jit(solution)/shard_map/add | solution.py:174
  78.0 0.7 copy.142
  (81 shorter events, 5.3 us)
Async XLA Ops:
  0.6 4.6 %copy-start.3 = (f32[19,4,8,128]{3,2,1,0:T(8,128)S(1)}, f32[19,4,8,128]{3,2,1,0:T(8,128)}, u32[]{:S(2)}) copy-start(f32[19,4,8,128]{3,2,1,0:T(8,128)} %param.9) | copy-start | bytes 933892
  2.1 3.2 %copy-start.2 = (f32[4,8,128]{2,1,0:T(8,128)S(1)}, f32[4,8,128]{2,1,0:T(8,128)}, u32[]{:S(2)}) copy-start(f32[4,8,128]{2,1,0:T(8,128)} %param.6) | copy-start | bytes 49156
  5.7 18.1 %collective-permute-start = (f32[40,2,8,128]{3,1,2,0:T(2,128)S(1)}, f32[40,2,8,128]{3,1,2,0:T(2,128)S(1)}, u32[]{:S(2)}, u32[]{:S(2)}) collective-permute-start(f32[40,2,8,128]{3,1,2,0:T(2,128)S(1)} %get-tuple-element.121), channel_id=1, source_target_pairs={{0,1},{1,2},{2,3},{3,4},{4,5},{5,6},{6,7},{7,0},{8,9},{9,10},{10,1... | collective-permute-start | bytes 983048 | tf_op jit(solution)/shard_map/ppermute | solution.py:134
  9.7 15.0 %collective-permute-start.1 = (f32[40,2,8,128]{3,1,2,0:T(2,128)S(1)}, f32[40,2,8,128]{3,1,2,0:T(2,128)S(1)}, u32[]{:S(2)}, u32[]{:S(2)}) collective-permute-start(f32[40,2,8,128]{3,1,2,0:T(2,128)S(1)} %get-tuple-element.122), channel_id=1, source_target_pairs={{1,0},{2,1},{3,2},{4,3},{5,4},{6,5},{7,6},{0,7},{9,8},{10,9},{11,1... | collective-permute-start | bytes 983048 | tf_op jit(solution)/shard_map/ppermute | solution.py:137
  24.8 9.6 %collective-permute-start.2 = (f32[40,8,2,128]{3,1,2,0:T(8,128)S(1)}, f32[40,8,2,128]{3,1,2,0:T(8,128)S(1)}, u32[]{:S(2)}, u32[]{:S(2)}) collective-permute-start(f32[40,8,2,128]{3,1,2,0:T(8,128)S(1)} %get-tuple-element.119), channel_id=1, source_target_pairs={{0,8},{8,16},{16,24},{24,32},{32,40},{40,48},{48,56},{56,0},{1,9},... | collective-permute-start | bytes 983048 | tf_op jit(solution)/shard_map/ppermute | solution.py:134
  28.0 11.4 %collective-permute-start.3 = (f32[40,8,2,128]{3,1,2,0:T(8,128)S(1)}, f32[40,8,2,128]{3,1,2,0:T(8,128)S(1)}, u32[]{:S(2)}, u32[]{:S(2)}) collective-permute-start(f32[40,8,2,128]{3,1,2,0:T(8,128)S(1)} %get-tuple-element.120), channel_id=1, source_target_pairs={{8,0},{16,8},{24,16},{32,24},{40,32},{48,40},{56,48},{0,56},{9,1},... | collective-permute-start | bytes 983048 | tf_op jit(solution)/shard_map/ppermute | solution.py:137
  34.4 5.0 %copy-start = (f32[40,8,2,128]{3,1,2,0:T(8,128)}, f32[40,8,2,128]{3,1,2,0:T(8,128)S(1)}, u32[]{:S(2)}) copy-start(f32[40,8,2,128]{3,1,2,0:T(8,128)S(1)} %collective-permute-done.2) | copy-start | bytes 983044
  39.4 0.7 copy-start.1
  45.1 11.0 %collective-permute-start.4 = (f32[40,8,12,2]{0,1,3,2:T(8,128)S(1)}, f32[40,8,12,2]{0,1,3,2:T(8,128)S(1)}, u32[]{:S(2)}, u32[]{:S(2)}) collective-permute-start(f32[40,8,12,2]{0,1,3,2:T(8,128)S(1)} %copy.137), channel_id=1, source_target_pairs={{0,64},{64,128},{128,192},{192,256},{256,320},{320,384},{384,448},... | collective-permute-start | bytes 92168 | tf_op jit(solution)/shard_map/ppermute | solution.py:134
  53.9 9.4 %collective-permute-start.5 = (f32[40,8,12,2]{0,1,3,2:T(8,128)}, f32[40,8,12,2]{0,1,3,2:T(8,128)}, u32[]{:S(2)}, u32[]{:S(2)}) collective-permute-start(f32[40,8,12,2]{0,1,3,2:T(8,128)} %copy.138), channel_id=1, source_target_pairs={{64,0},{128,64},{192,128},{256,192},{320,256},{384,320},{448,384},... | collective-permute-start | bytes 92168 | tf_op jit(solution)/shard_map/ppermute | solution.py:137
  75.0 0.7 copy-start.5
  75.2 2.1 %copy-start.4 = (s32[4,8,128]{2,1,0:T(8,128)S(1)}, s32[4,8,128]{2,1,0:T(8,128)}, u32[]{:S(2)}) copy-start(s32[4,8,128]{2,1,0:T(8,128)} %param.7) | copy-start | bytes 49156

commit v2 on v1

v2 whole, which is shorter than its diff:
```python
import math

import jax
import jax.numpy as jnp
from jax import lax
from jax.experimental import pallas as pl
from jax.experimental.pallas import tpu as pltpu
from jax.sharding import PartitionSpec as P

VELOCITIES = (
    (0, 0, 0),
    (1, 0, 0),
    (-1, 0, 0),
    (0, 1, 0),
    (0, -1, 0),
    (0, 0, 1),
    (0, 0, -1),
    (1, 1, 0),
    (-1, -1, 0),
    (1, -1, 0),
    (-1, 1, 0),
    (1, 0, 1),
    (-1, 0, -1),
    (1, 0, -1),
    (-1, 0, 1),
    (0, 1, 1),
    (0, -1, -1),
    (0, 1, -1),
    (0, -1, 1),
)
WEIGHTS = (1.0 / 3.0,) + (1.0 / 18.0,) * 6 + (1.0 / 36.0,) * 12
OPPOSITE = (0, 2, 1, 4, 3, 6, 5, 8, 7, 10, 9, 12, 11, 14, 13, 16, 15, 18, 17)
Q = 19
RATE = 1.25
RAMP = 0.1
NZ, NY, NX = 4, 8, 128
EXT = NZ + 2
LOW, HIGH = EXT, EXT + 1
SIDES = EXT + 2
ROWS = 8

FORWARD, ADJOINT, DESIGN, KIND = range(4)


def opposed(c):
    return tuple(-i for i in c)


Z_FIELDS = (
    [(FORWARD, q, VELOCITIES[q][2]) for q in range(Q)]
    + [(ADJOINT, q, -VELOCITIES[q][2]) for q in range(Q)]
    + [(DESIGN, 0, 0), (KIND, 0, 0)]
)
Z_UP, Z_DOWN = [], []
for _what, _which, _s in Z_FIELDS:
    if _s >= 0:
        Z_UP += [(_what, _which, p) for p in range(NZ - 1 - _s, NZ)]
    if _s <= 0:
        Z_DOWN += [(_what, _which, p) for p in range(0, 1 - _s)]
Z_UP_AT = {entry: i for i, entry in enumerate(Z_UP)}
Z_DOWN_AT = {entry: i for i, entry in enumerate(Z_DOWN)}

Y_FIELDS = []
for _cy in (-1, 0, 1):
    for _cx in (-1, 0, 1):
        _same = [q for q in range(Q) if VELOCITIES[q][:2] == (_cx, _cy)]
        Y_FIELDS.append((FORWARD, (_cx, _cy, 0), [(1, q) for q in _same], _cy))
        _deep = [(VELOCITIES[q][2], q) for q in _same if VELOCITIES[q][2]]
        if _deep:
            Y_FIELDS.append((FORWARD, (_cx, _cy, 1), _deep, _cy))
Y_FIELDS += [(ADJOINT, q, [(1, q)], -VELOCITIES[q][1]) for q in range(Q)]
Y_FIELDS += [(DESIGN, 0, [(1, 0)], 0), (KIND, 0, [(1, 0)], 0)]
Y_AT = {(what, which): i for i, (what, which, _, _) in enumerate(Y_FIELDS)}
Y_UP, Y_DOWN = [], []
for _i, (_, _, _, _s) in enumerate(Y_FIELDS):
    if _s >= 0:
        Y_UP += [(_i, row) for row in range(NY - 1 - _s, NY)]
    if _s <= 0:
        Y_DOWN += [(_i, row) for row in range(0, 1 - _s)]
Y_UP_AT = {entry: i for i, entry in enumerate(Y_UP)}
Y_DOWN_AT = {entry: i for i, entry in enumerate(Y_DOWN)}


def padded(rows):
    return -(-(rows + 2) // ROWS) * ROWS


Y_UP_ROWS, Y_DOWN_ROWS = padded(len(Y_UP) * EXT), padded(len(Y_DOWN) * EXT)

X_FIELDS = []
for _s in (1, -1, 0):
    X_FIELDS += [(FORWARD, (_s, i)) for i in range(3)]
    X_FIELDS += [(ADJOINT, q) for q in range(Q) if -VELOCITIES[q][0] == _s]
X_FIELDS += [(DESIGN, 0), (KIND, 0)]
X_AT = {entry: i for i, entry in enumerate(X_FIELDS)}
PER_TILE = 4
PACKED = -(-len(X_FIELDS) // PER_TILE)


def shift_of(entry):
    what, which = entry
    if what == FORWARD:
        return which[0]
    return -VELOCITIES[which][0] if what == ADJOINT else 0


def add_up(terms):
    total = None
    for sign, value in terms:
        if total is None:
            total = value if sign > 0 else -value
        else:
            total = total + value if sign > 0 else total - value
    return total


def moments(f):
    density = add_up([(1, f[q]) for q in range(Q)])
    flow = [
        add_up([(VELOCITIES[q][i], f[q]) for q in range(Q) if VELOCITIES[q][i]])
        for i in range(3)
    ]
    return density, flow


def along(q, vector):
    return add_up([(VELOCITIES[q][i], vector[i]) for i in range(3) if VELOCITIES[q][i]])


def collide(f, porosity, kinds, speed):
    density, flow = moments(f)
    inverse = 1.0 / density
    fluid = kinds == 0
    wall = kinds == 1
    inlet = kinds == 2
    damping = RAMP * (1.0 - porosity) / (RAMP + porosity)
    kept = jnp.where(fluid, 1.0 - damping, 1.0)
    v = [
        jnp.where(inlet, speed if i == 0 else 0.0, flow[i] * inverse * kept)
        for i in range(3)
    ]
    r = jnp.where(inlet, 1.0, density)
    scale = jnp.where(fluid, RATE, 1.0) * r
    keep = jnp.where(fluid, 1.0 - RATE, 0.0)
    base = 1.0 - 1.5 * (v[0] * v[0] + v[1] * v[1] + v[2] * v[2])
    out = []
    for q in range(Q):
        p = along(q, v)
        shape = base if p is None else base + p * (3.0 + 4.5 * p)
        moved = keep * f[q] + (WEIGHTS[q] * scale) * shape
        out.append(jnp.where(wall, f[OPPOSITE[q]], moved))
    return out


def pull_back(density, flow, h, porosity, kinds, wanted):
    fluid = kinds == 0
    wall = kinds == 1
    outlet = kinds == 3
    inverse = 1.0 / density
    u = [flow[i] * inverse for i in range(3)]
    square = u[0] * u[0] + u[1] * u[1] + u[2] * u[2]
    ramp = 1.0 / (RAMP + porosity)
    damping = jnp.where(fluid, RAMP * (1.0 - porosity) * ramp, 0.0)
    kept = 1.0 - damping
    v = [kept * u[i] for i in range(3)]
    face, edge = WEIGHTS[1], WEIGHTS[7]
    plus = {}
    minus = {}
    for q in range(1, Q, 2):
        plus[q] = h[q] + h[q + 1]
        minus[q] = h[q] - h[q + 1]
    xy, yx, xz, zx, yz, zy = (plus[q] for q in (7, 9, 11, 13, 15, 17))
    second = [
        [face * plus[1] + edge * ((xy + yx) + (xz + zx)), edge * (xy - yx), edge * (xz - zx)],
        [None, face * plus[3] + edge * ((xy + yx) + (yz + zy)), edge * (yz - zy)],
        [None, None, face * plus[5] + edge * ((xz + zx) + (yz + zy))],
    ]
    second[1][0], second[2][0], second[2][1] = second[0][1], second[0][2], second[1][2]
    zero = (
        WEIGHTS[0] * h[0]
        + face * (plus[1] + plus[3] + plus[5])
        + edge * ((xy + yx) + (xz + zx) + (yz + zy))
    )
    first = [
        face * minus[1] + edge * ((minus[7] + minus[9]) + (minus[11] + minus[13])),
        face * minus[3] + edge * ((minus[7] - minus[9]) + (minus[15] + minus[17])),
        face * minus[5] + edge * ((minus[11] - minus[13]) + (minus[15] - minus[17])),
    ]
    bent = [
        4.5 * (second[i][0] * v[0] + second[i][1] * v[1] + second[i][2] * v[2])
        - 1.5 * zero * v[i]
        for i in range(3)
    ]
    level = zero + sum(v[i] * (3.0 * first[i] + bent[i]) for i in range(3))
    slope = [3.0 * first[i] + 2.0 * bent[i] for i in range(3)]
    rate = jnp.where(fluid, RATE, jnp.where(outlet, 1.0, 0.0))
    keep = jnp.where(fluid, 1.0 - RATE, 0.0)
    turn = sum(slope[i] * u[i] for i in range(3))
    moved_rate = rate * kept
    tilt = [moved_rate * slope[i] + 2.0 * damping * u[i] for i in range(3)]
    flat = rate * level - moved_rate * turn - damping * square
    out = {}
    for q in wanted:
        p = along(q, tilt)
        moved = keep * h[q] + (flat if p is None else flat + p)
        out[q] = jnp.where(wall, h[OPPOSITE[q]], moved)
    by_porosity = jnp.where(
        fluid,
        (-RAMP * (1.0 + RAMP)) * ramp * ramp * density * (square - RATE * turn),
        0.0,
    )
    return out, by_porosity


def collide_kernel(step, pop, adj, por, kind, moved, up, down):
    moment = jnp.full((NY, NX), step[0] & 63, jnp.int32).astype(jnp.float32)
    speed = 0.1 * (1.0 + 0.8 * jnp.sin((2.0 * math.pi / 64.0) * moment))
    for z in range(NZ):
        kinds = kind[z]
        design = por[z]
        collided = collide([pop[q, z] for q in range(Q)], design, kinds, speed)
        for q in range(Q):
            moved[q, z] = collided[q]

        def value(what, which):
            if what == FORWARD:
                return collided[which]
            if what == ADJOINT:
                return adj[which, z]
            return design if what == DESIGN else kinds.astype(jnp.float32)

        for table, out in ((Z_UP_AT, up), (Z_DOWN_AT, down)):
            for (what, which, plane), at in table.items():
                if plane == z:
                    out[at] = value(what, which)


def rows_kernel(moved, adj, por, kind, below, above, shifted, up, down):
    def plane_of(what, which, z):
        if z < 0:
            return below[Z_UP_AT[what, which, z + NZ]]
        if z >= NZ:
            return above[Z_DOWN_AT[what, which, z - NZ]]
        if what == FORWARD:
            return moved[which, z]
        if what == ADJOINT:
            return adj[which, z]
        return por[z] if what == DESIGN else kind[z].astype(jnp.float32)

    for i, (what, _, parts, _) in enumerate(Y_FIELDS):
        for t in range(EXT):
            terms = []
            for sign, q in parts:
                s = VELOCITIES[q][2] if what == FORWARD else 0
                if what == ADJOINT:
                    s = -VELOCITIES[q][2]
                terms.append((sign, plane_of(what, q, t - 1 - s)))
            shifted[pl.ds((i * EXT + t) * ROWS, ROWS), :] = add_up(terms)
    for table, out in ((Y_UP, up), (Y_DOWN, down)):
        for at, (i, row) in enumerate(table):
            out[pl.ds(at * EXT, EXT), :] = shifted[
                pl.ds(i * EXT * ROWS + row, EXT, stride=ROWS), :
            ]
        used = len(table) * EXT
        out[pl.ds(used, out.shape[0] - used), :] = jnp.zeros(
            (out.shape[0] - used, NX), jnp.float32
        )


def columns_kernel(shifted, up, down, left, right, wide, packed):
    row = lax.broadcasted_iota(jnp.int32, (NY, NX), 0)
    lane = lax.broadcasted_iota(jnp.int32, (NY, NX), 1)

    def rows_of(ref, at):
        return ref[pl.ds(at * EXT, ROWS), :]

    def row_of(ref, at, t):
        return jnp.broadcast_to(ref[pl.ds(at * EXT + t, 1), :], (NY, NX))

    def tile_of(entry, t):
        i = Y_AT[entry]
        s = Y_FIELDS[i][3]
        if t == LOW:
            if s < 0:
                return rows_of(down, Y_DOWN_AT[i, 0])
            return rows_of(left, Y_UP_AT[i, NY - 1 - s])
        if t == HIGH:
            if s > 0:
                return rows_of(up, Y_UP_AT[i, NY - 1])
            return rows_of(right, Y_DOWN_AT[i, -s])
        own = shifted[pl.ds((i * EXT + t) * ROWS, ROWS), :]
        if s > 0:
            return jnp.where(
                row == 0, row_of(left, Y_UP_AT[i, NY - 1], t), pltpu.roll(own, 1, 0)
            )
        if s < 0:
            return jnp.where(
                row == NY - 1, row_of(right, Y_DOWN_AT[i, 0], t), pltpu.roll(own, NY - 1, 0)
            )
        return own

    for u in range(PACKED):
        total = None
        for j, entry in enumerate(X_FIELDS[u * PER_TILE : (u + 1) * PER_TILE]):
            f = u * PER_TILE + j
            what, which = entry
            for t in range(EXT + 2):
                if what != FORWARD:
                    tile = tile_of(entry, t)
                else:
                    cx, part = which
                    terms = []
                    for cy in (-1, 0, 1):
                        source = (FORWARD, (cx, cy, 1 if part == 2 else 0))
                        if source in Y_AT and (part != 1 or cy):
                            sign = cy if part == 1 else 1
                            terms.append((sign, tile_of(source, t)))
                    tile = add_up(terms)
                wide[pl.ds((f * (EXT + 2) + t) * ROWS, ROWS), :] = tile
                k = j * (EXT + 2) + t
                turned = pltpu.roll(tile, (2 + 4 * k) % NX, 1)
                total = turned if total is None else jnp.where(lane >= 4 * k, turned, total)
        packed[u] = total


def adjoint_kernel(wide, packed, before, after, pop, por, kind, out, sense, states):
    lane = lax.broadcasted_iota(jnp.int32, (NY, NX), 1)
    row = lax.broadcasted_iota(jnp.int32, (NY, NX), 0)
    slot = lane & 3
    beside = [jnp.where(slot < 2, before[u], after[u]) for u in range(PACKED)]

    def value(entry, t):
        f = X_AT[entry]
        u, j = f // PER_TILE, f % PER_TILE
        s = shift_of(entry)
        if t == SIDES:
            if s > 0:
                base = jnp.where(slot == 1, pltpu.roll(beside[u], 1, 1), pltpu.roll(packed[u], 1, 1))
            elif s < 0:
                base = jnp.where(
                    slot == 2, pltpu.roll(beside[u], NX - 1, 1), pltpu.roll(packed[u], NX - 1, 1)
                )
            else:
                base = beside[u]
            return pltpu.roll(base, NX - 32 * j, 1) if j else base
        own = wide[pl.ds((f * (EXT + 2) + t) * ROWS, ROWS), :]
        k = j * (EXT + 2) + t
        if s > 0:
            return jnp.where(
                lane == 0, pltpu.roll(beside[u], NX - (4 * k + 1), 1), pltpu.roll(own, 1, 1)
            )
        if s < 0:
            return jnp.where(
                lane == NX - 1,
                pltpu.roll(beside[u], (NX - 1 - (4 * k + 2)) % NX, 1),
                pltpu.roll(own, NX - 1, 1),
            )
        return own

    def at(q, t):
        return pl.ds((q * (SIDES + 1) + t) * ROWS, ROWS)

    for t in (SIDES, LOW, HIGH, 0, EXT - 1, *range(1, NZ + 1)):
        if t == SIDES:
            wanted = [q for q in range(Q) if VELOCITIES[q][0]]
        elif t in (LOW, HIGH):
            wanted = [q for q in range(Q) if VELOCITIES[q][1] == (1 if t == HIGH else -1)]
        elif t in (0, EXT - 1):
            wanted = [q for q in range(Q) if VELOCITIES[q][2] == (1 if t else -1)]
        else:
            wanted = range(Q)
        parts = {s: [value((FORWARD, (s, i)), t) for i in range(3)] for s in (-1, 0, 1)}
        density = parts[0][0] + parts[1][0] + parts[-1][0]
        flow = [
            parts[1][0] - parts[-1][0],
            parts[0][1] + parts[1][1] + parts[-1][1],
            parts[0][2] + parts[1][2] + parts[-1][2],
        ]
        h = [value((ADJOINT, q), t) for q in range(Q)]
        back, by_porosity = pull_back(
            density, flow, h, value((DESIGN, 0), t), value((KIND, 0), t), wanted
        )
        for q in wanted:
            states[at(q, t), :] = back[q]
        if 1 <= t <= NZ:
            sense[t - 1] = by_porosity

    def moved_x(q, t):
        tile = states[at(q, t), :]
        cx = VELOCITIES[q][0]
        if cx > 0:
            return jnp.where(
                lane == NX - 1,
                pltpu.roll(states[at(q, SIDES), :], (NX - 1 - (4 * t + 2)) % NX, 1),
                pltpu.roll(tile, NX - 1, 1),
            )
        if cx < 0:
            return jnp.where(
                lane == 0,
                pltpu.roll(states[at(q, SIDES), :], NX - (4 * t + 1), 1),
                pltpu.roll(tile, 1, 1),
            )
        return tile

    for z in range(NZ):
        h = []
        for q in range(Q):
            _, cy, cz = VELOCITIES[q]
            t = z + cz + 1
            tile = moved_x(q, t)
            if cy > 0:
                edge = moved_x(q, HIGH)[t : t + 1]
                tile = jnp.where(
                    row == NY - 1, jnp.broadcast_to(edge, (NY, NX)), pltpu.roll(tile, NY - 1, 0)
                )
            elif cy < 0:
                edge = moved_x(q, LOW)[t : t + 1]
                tile = jnp.where(row == 0, jnp.broadcast_to(edge, (NY, NX)), pltpu.roll(tile, 1, 0))
            h.append(tile)
        density, flow = moments([pop[q, z] for q in range(Q)])
        back, by_porosity = pull_back(
            density, flow, h, por[z], kind[z].astype(jnp.float32), range(Q)
        )
        for q in range(Q):
            out[q, z] = back[q]
        sense[z] = sense[z] + by_porosity


VMEM = pl.BlockSpec(memory_space=pltpu.VMEM)
SMEM = pl.BlockSpec(memory_space=pltpu.SMEM)


def call(kernel, shapes, specs, scratch=()):
    out = [jax.ShapeDtypeStruct(shape, jnp.float32) for shape in shapes]
    return pl.pallas_call(
        kernel,
        out_shape=out,
        in_specs=specs,
        out_specs=[VMEM] * len(out),
        scratch_shapes=list(scratch),
        compiler_params=pltpu.CompilerParams(vmem_limit_bytes=12 * 1024 * 1024),
    )


def both_ways(forward, backward, axis):
    count = lax.axis_size(axis)
    ahead = [(i, (i + 1) % count) for i in range(count)]
    behind = [(t, s) for s, t in ahead]
    return lax.ppermute(forward, axis, ahead), lax.ppermute(backward, axis, behind)


def on_device(populations, porosity, node_type, step_index, adjoint_end):
    tile = (NY, NX)
    moved, up, down = call(
        collide_kernel,
        [(Q, NZ, *tile), (len(Z_UP), *tile), (len(Z_DOWN), *tile)],
        [SMEM] + [VMEM] * 4,
    )(step_index, populations, adjoint_end, porosity, node_type)
    below, above = both_ways(up, down, "gz")
    shifted, up, down = call(
        rows_kernel,
        [(len(Y_FIELDS) * EXT * ROWS, NX), (Y_UP_ROWS, NX), (Y_DOWN_ROWS, NX)],
        [VMEM] * 6,
    )(moved, adjoint_end, porosity, node_type, below, above)
    left, right = both_ways(up, down, "gy")
    wide, packed = call(
        columns_kernel,
        [(len(X_FIELDS) * (EXT + 2) * ROWS, NX), (PACKED, *tile)],
        [VMEM] * 5,
    )(shifted, up, down, left, right)
    before, after = both_ways(packed, packed, "gx")
    adjoint, sense = call(
        adjoint_kernel,
        [(Q, NZ, *tile), (NZ, *tile)],
        [VMEM] * 7,
        [pltpu.VMEM((Q * (SIDES + 1) * ROWS, NX), jnp.float32)],
    )(wide, packed, before, after, populations, porosity, node_type)
    return adjoint, sense


def solution(mesh):
    brick = P(None, "gz", "gy", "gx")
    field = P("gz", "gy", "gx")
    return jax.shard_map(
        on_device,
        mesh=mesh,
        in_specs=(brick, field, field, P(), brick),
        out_specs=(brick, field),
        check_vma=False,
    )
```

time: 79.4 us -> 45.5 us (0.57)
  the two profiles are of different devices: /device:TPU:23 before, /device:TPU:14 now
where the time goes in v2:
time: 45.5 us; the launch traced here: 45 us
  starting transfers between devices  23.9 us (53%)
  waiting for transfers between devices  14.4 us (32%)
  local copies, waits for them, and re-layouts  3.37 us (7%)
  Pallas kernels  1.99 us (4%)
  between operations  1.36 us (3%)
    ppermute x3, starting transfers between devices, both_ways(): lax.ppermute(backward, axis, behind)  15.5 us
    ppermute x3, waiting for transfers between devices, both_ways(): lax.ppermute(forward, axis, ahead)  8.79 us
    ppermute x3, starting transfers between devices, both_ways(): lax.ppermute(forward, axis, ahead)  8.47 us
    ppermute x3, waiting for transfers between devices, both_ways(): lax.ppermute(backward, axis, behind)  5.57 us
    unnamed x12, local copies, waits for them, and re-layouts  3.37 us
    pallas_call x1, Pallas kernels, on_device(): call(adjoint_kernel, [(Q, NZ, *tile), (NZ, *tile)], [VMEM] * 7, [pltpu.VM...  1.37 us
  transfers between devices with their start and end apart: 6, of which 5 were waited for; matrix products, arithmetic and copies ran while one was open for 0% of the time, Pallas kernels for 0%

profile of v2, /device:TPU:14, one launch (start us, length us, event | category | flops | bytes accessed | tf_op | source)
XLA Modules:
  0.0 45.0 jit_solution(714054705533031724)
XLA Ops:
  1.3 0.0 copy-start
  1.3 1.0 %copy-done = f32[19,4,8,128]{3,2,1,0:T(8,128)S(1)} copy-done((f32[19,4,8,128]{3,2,1,0:T(8,128)S(1)}, f32[19,4,8,128]{3,2,1,0:T(8,128)}, u32[]{:S(2)}) %copy-start) | copy-done | bytes 311320
  2.2 0.0 copy-start.2
  2.2 1.0 %copy-done.2 = f32[19,4,8,128]{3,2,1,0:T(8,128)S(1)} copy-done((f32[19,4,8,128]{3,2,1,0:T(8,128)S(1)}, f32[19,4,8,128]{3,2,1,0:T(8,128)}, u32[]{:S(2)}) %copy-start.2) | copy-done | bytes 311320
  3.2 0.7 %copy-done.4 = f32[4,8,128]{2,1,0:T(8,128)S(1)} copy-done((f32[4,8,128]{2,1,0:T(8,128)S(1)}, f32[4,8,128]{2,1,0:T(8,128)}, u32[]{:S(2)}) %copy-start.4) | copy-done | bytes 16408
  3.9 0.7 %copy-done.5 = s32[4,8,128]{2,1,0:T(8,128)S(1)} copy-done((s32[4,8,128]{2,1,0:T(8,128)S(1)}, s32[4,8,128]{2,1,0:T(8,128)}, u32[]{:S(2)}) %copy-start.5) | copy-done | bytes 16408
  4.7 0.2 shard_map.68
  4.8 4.3 %collective-permute-start = (f32[40,8,128]{2,1,0:T(8,128)S(1)}, f32[40,8,128]{2,1,0:T(8,128)S(1)}, u32[]{:S(2)}, u32[]{:S(2)}) collective-permute-start(f32[40,8,128]{2,1,0:T(8,128)S(1)} %get-tuple-element.11), channel_id=1, source_target_pairs={{0,1},{1,2},{2,3},{3,4},{4,5},{5,6},{6,7},{7,0},{8,9},{9,10},{10,1... | collective-permute-start | bytes 491528 | tf_op jit(solution)/shard_map/ppermute | solution.py:449
  9.1 8.6 %collective-permute-start.1 = (f32[40,8,128]{2,1,0:T(8,128)S(1)}, f32[40,8,128]{2,1,0:T(8,128)S(1)}, u32[]{:S(2)}, u32[]{:S(2)}) collective-permute-start(f32[40,8,128]{2,1,0:T(8,128)S(1)} %get-tuple-element.12), channel_id=1, source_target_pairs={{1,0},{2,1},{3,2},{4,3},{5,4},{6,5},{7,6},{0,7},{9,8},{10,9},{11,1... | collective-permute-start | bytes 491528 | tf_op jit(solution)/shard_map/ppermute | solution.py:449
  17.7 2.3 %collective-permute-done.below = f32[40,8,128]{2,1,0:T(8,128)S(1)} collective-permute-done((f32[40,8,128]{2,1,0:T(8,128)S(1)}, f32[40,8,128]{2,1,0:T(8,128)S(1)}, u32[]{:S(2)}, u32[]{:S(2)}) %collective-permute-start) | collective-permute-done | bytes 163872 | tf_op jit(solution)/shard_map/ppermute | solution.py:449
  20.0 1.2 %collective-permute-done.1.above = f32[40,8,128]{2,1,0:T(8,128)S(1)} collective-permute-done((f32[40,8,128]{2,1,0:T(8,128)S(1)}, f32[40,8,128]{2,1,0:T(8,128)S(1)}, u32[]{:S(2)}, u32[]{:S(2)}) %collective-permute-start.1) | collective-permute-done | bytes 163872 | tf_op jit(solution)/shard_map/ppermute | solution.py:449
  21.1 0.0 copy-done.1
  21.1 0.1 shard_map.69
  21.3 2.3 %collective-permute-start.2 = (f32[216,128]{1,0:T(8,128)S(1)}, f32[216,128]{1,0:T(8,128)S(1)}, u32[]{:S(2)}, u32[]{:S(2)}) collective-permute-start(f32[216,128]{1,0:T(8,128)S(1)} %get-tuple-element.14.up), channel_id=1, source_target_pairs={{0,8},{8,16},{16,24},{24,32},{32,40},{40,48},{48,56},{56,0},{1,9},... | collective-permute-start | bytes 331784 | tf_op jit(solution)/shard_map/ppermute | solution.py:449
  23.5 3.6 %collective-permute-start.3 = (f32[216,128]{1,0:T(8,128)S(1)}, f32[216,128]{1,0:T(8,128)S(1)}, u32[]{:S(2)}, u32[]{:S(2)}) collective-permute-start(f32[216,128]{1,0:T(8,128)S(1)} %get-tuple-element.15.down), channel_id=1, source_target_pairs={{8,0},{16,8},{24,16},{32,24},{40,32},{48,40},{56,48},{0,56},{9,1},... | collective-permute-start | bytes 331784 | tf_op jit(solution)/shard_map/ppermute | solution.py:449
  27.1 0.8 %collective-permute-done.2.left = f32[216,128]{1,0:T(8,128)S(1)} collective-permute-done((f32[216,128]{1,0:T(8,128)S(1)}, f32[216,128]{1,0:T(8,128)S(1)}, u32[]{:S(2)}, u32[]{:S(2)}) %collective-permute-start.2) | collective-permute-done | bytes 110624 | tf_op jit(solution)/shard_map/ppermute | solution.py:449
  27.9 4.4 %collective-permute-done.3.right = f32[216,128]{1,0:T(8,128)S(1)} collective-permute-done((f32[216,128]{1,0:T(8,128)S(1)}, f32[216,128]{1,0:T(8,128)S(1)}, u32[]{:S(2)}, u32[]{:S(2)}) %collective-permute-start.3) | collective-permute-done | bytes 110624 | tf_op jit(solution)/shard_map/ppermute | solution.py:449
  32.3 0.3 shard_map.70
  32.6 3.3 %collective-permute-start.5 = (f32[8,8,128]{2,1,0:T(8,128)S(1)}, f32[8,8,128]{2,1,0:T(8,128)S(1)}, u32[]{:S(2)}, u32[]{:S(2)}) collective-permute-start(f32[8,8,128]{2,1,0:T(8,128)S(1)} %get-tuple-element.17.packed), channel_id=1, source_target_pairs={{64,0},{128,64},{192,128},{256,192},{320,256},{384,320},{448,384},... | collective-permute-start | bytes 98312 | tf_op jit(solution)/shard_map/ppermute | solution.py:449
  36.0 1.9 %collective-permute-start.4 = (f32[8,8,128]{2,1,0:T(8,128)S(1)}, f32[8,8,128]{2,1,0:T(8,128)S(1)}, u32[]{:S(2)}, u32[]{:S(2)}) collective-permute-start(f32[8,8,128]{2,1,0:T(8,128)S(1)} %get-tuple-element.17.packed), channel_id=1, source_target_pairs={{0,64},{64,128},{128,192},{192,256},{256,320},{320,384},{384,448},... | collective-permute-start | bytes 98312 | tf_op jit(solution)/shard_map/ppermute | solution.py:449
  37.9 0.0 collective-permute-done.5.after
  37.9 5.8 %collective-permute-done.4.before = f32[8,8,128]{2,1,0:T(8,128)S(1)} collective-permute-done((f32[8,8,128]{2,1,0:T(8,128)S(1)}, f32[8,8,128]{2,1,0:T(8,128)S(1)}, u32[]{:S(2)}, u32[]{:S(2)}) %collective-permute-start.4) | collective-permute-done | bytes 32800 | tf_op jit(solution)/shard_map/ppermute | solution.py:449
  43.6 0.0 copy-done.3
  43.7 1.4 %shard_map.71 = (f32[19,4,8,128]{3,2,1,0:T(8,128)}, f32[4,8,128]{2,1,0:T(8,128)}) custom-call(f32[1920,128]{1,0:T(8,128)S(1)} %get-tuple-element.16.wide, f32[8,8,128]{2,1,0:T(8,128)S(1)} %get-tuple-element.17.packed, f32[8,8,128]{2,1,0:T(8,128)S(1)} %collective-permute-done.4.before, f32[8,8,128]{2,1,0:T(8,128)S(1)} %collective-permute-done.5.after, ...), custom_call_target="tpu_custom_call" | custom-call | tf_op jit(solution)/shard_map/pallas_call | solution.py:472
  (4 shorter events, 0.0 us)
Async XLA Ops:
  1.3 1.0 %copy-start = (f32[19,4,8,128]{3,2,1,0:T(8,128)S(1)}, f32[19,4,8,128]{3,2,1,0:T(8,128)}, u32[]{:S(2)}) copy-start(f32[19,4,8,128]{3,2,1,0:T(8,128)} %adj.3) | copy-start | bytes 933892
  2.2 1.0 %copy-start.2 = (f32[19,4,8,128]{3,2,1,0:T(8,128)S(1)}, f32[19,4,8,128]{3,2,1,0:T(8,128)}, u32[]{:S(2)}) copy-start(f32[19,4,8,128]{3,2,1,0:T(8,128)} %pop.3) | copy-start | bytes 933892
  3.2 0.7 %copy-start.4 = (f32[4,8,128]{2,1,0:T(8,128)S(1)}, f32[4,8,128]{2,1,0:T(8,128)}, u32[]{:S(2)}) copy-start(f32[4,8,128]{2,1,0:T(8,128)} %por.5) | copy-start | bytes 49156
  3.9 0.7 %copy-start.5 = (s32[4,8,128]{2,1,0:T(8,128)S(1)}, s32[4,8,128]{2,1,0:T(8,128)}, u32[]{:S(2)}) copy-start(s32[4,8,128]{2,1,0:T(8,128)} %kind.5) | copy-start | bytes 49156
  4.6 16.5 %copy-start.1 = (f32[19,4,8,128]{3,2,1,0:T(8,128)S(1)}, f32[19,4,8,128]{3,2,1,0:T(8,128)}, u32[]{:S(2)}) copy-start(f32[19,4,8,128]{3,2,1,0:T(8,128)} %adj.3) | copy-start | bytes 933892
  4.8 15.1 %collective-permute-start = (f32[40,8,128]{2,1,0:T(8,128)S(1)}, f32[40,8,128]{2,1,0:T(8,128)S(1)}, u32[]{:S(2)}, u32[]{:S(2)}) collective-permute-start(f32[40,8,128]{2,1,0:T(8,128)S(1)} %get-tuple-element.11), channel_id=1, source_target_pairs={{0,1},{1,2},{2,3},{3,4},{4,5},{5,6},{6,7},{7,0},{8,9},{9,10},{10,1... | collective-permute-start | bytes 491528 | tf_op jit(solution)/shard_map/ppermute | solution.py:449
  9.1 12.0 %collective-permute-start.1 = (f32[40,8,128]{2,1,0:T(8,128)S(1)}, f32[40,8,128]{2,1,0:T(8,128)S(1)}, u32[]{:S(2)}, u32[]{:S(2)}) collective-permute-start(f32[40,8,128]{2,1,0:T(8,128)S(1)} %get-tuple-element.12), channel_id=1, source_target_pairs={{1,0},{2,1},{3,2},{4,3},{5,4},{6,5},{7,6},{0,7},{9,8},{10,9},{11,1... | collective-permute-start | bytes 491528 | tf_op jit(solution)/shard_map/ppermute | solution.py:449
  21.3 6.6 %collective-permute-start.2 = (f32[216,128]{1,0:T(8,128)S(1)}, f32[216,128]{1,0:T(8,128)S(1)}, u32[]{:S(2)}, u32[]{:S(2)}) collective-permute-start(f32[216,128]{1,0:T(8,128)S(1)} %get-tuple-element.14.up), channel_id=1, source_target_pairs={{0,8},{8,16},{16,24},{24,32},{32,40},{40,48},{48,56},{56,0},{1,9},... | collective-permute-start | bytes 331784 | tf_op jit(solution)/shard_map/ppermute | solution.py:449
  23.5 8.8 %collective-permute-start.3 = (f32[216,128]{1,0:T(8,128)S(1)}, f32[216,128]{1,0:T(8,128)S(1)}, u32[]{:S(2)}, u32[]{:S(2)}) collective-permute-start(f32[216,128]{1,0:T(8,128)S(1)} %get-tuple-element.15.down), channel_id=1, source_target_pairs={{8,0},{16,8},{24,16},{32,24},{40,32},{48,40},{56,48},{0,56},{9,1},... | collective-permute-start | bytes 331784 | tf_op jit(solution)/shard_map/ppermute | solution.py:449
  32.3 11.4 %copy-start.3 = (f32[19,4,8,128]{3,2,1,0:T(8,128)S(1)}, f32[19,4,8,128]{3,2,1,0:T(8,128)}, u32[]{:S(2)}) copy-start(f32[19,4,8,128]{3,2,1,0:T(8,128)} %pop.3) | copy-start | bytes 933892
  32.6 5.2 %collective-permute-start.5 = (f32[8,8,128]{2,1,0:T(8,128)S(1)}, f32[8,8,128]{2,1,0:T(8,128)S(1)}, u32[]{:S(2)}, u32[]{:S(2)}) collective-permute-start(f32[8,8,128]{2,1,0:T(8,128)S(1)} %get-tuple-element.17.packed), channel_id=1, source_target_pairs={{64,0},{128,64},{192,128},{256,192},{320,256},{384,320},{448,384},... | collective-permute-start | bytes 98312 | tf_op jit(solution)/shard_map/ppermute | solution.py:449
  36.0 7.7 %collective-permute-start.4 = (f32[8,8,128]{2,1,0:T(8,128)S(1)}, f32[8,8,128]{2,1,0:T(8,128)S(1)}, u32[]{:S(2)}, u32[]{:S(2)}) collective-permute-start(f32[8,8,128]{2,1,0:T(8,128)S(1)} %get-tuple-element.17.packed), channel_id=1, source_target_pairs={{0,64},{64,128},{128,192},{192,256},{256,320},{320,384},{384,448},... | collective-permute-start | bytes 98312 | tf_op jit(solution)/shard_map/ppermute | solution.py:449

commit v3 on v2

--- a/solution.py
+++ b/solution.py
@@ -1,3 +1,4 @@
+import functools
 import math
 
 import jax
@@ -38,6 +39,7 @@
 LOW, HIGH = EXT, EXT + 1
 SIDES = EXT + 2
 ROWS = 8
+SWAPPED = ("gx",)
 
 FORWARD, ADJOINT, DESIGN, KIND = range(4)
 
@@ -212,35 +214,82 @@
     return out, by_porosity
 
 
-def collide_kernel(step, pop, adj, por, kind, moved, up, down):
+def by_side(axis, act, first, second):
+    if axis not in SWAPPED:
+        act(first, second)
+        return
+    here = lax.rem(lax.axis_index(axis), 2)
+
+    @pl.when(here == 0)
+    def _():
+        act(first, second)
+
+    @pl.when(here == 1)
+    def _():
+        act(second, first)
+
+
+def from_side(axis, first, second):
+    if axis not in SWAPPED:
+        return (lambda at: first[at]), (lambda at: second[at])
+    even = lax.rem(lax.axis_index(axis), 2) == 0
+    return (
+        lambda at: jnp.where(even, second[at], first[at]),
+        lambda at: jnp.where(even, first[at], second[at]),
+    )
+
+
+def collide_kernel(
+    step, pop_hbm, adj_hbm, por_hbm, kind_hbm, moved, first, second, pop, adj, por, kind, done
+):
+    copies = [
+        pltpu.make_async_copy(source, target, done.at[i])
+        for i, (source, target) in enumerate(
+            ((pop_hbm, pop), (por_hbm, por), (kind_hbm, kind), (adj_hbm, adj))
+        )
+    ]
+    for copy in copies:
+        copy.start()
     moment = jnp.full((NY, NX), step[0] & 63, jnp.int32).astype(jnp.float32)
     speed = 0.1 * (1.0 + 0.8 * jnp.sin((2.0 * math.pi / 64.0) * moment))
+    for copy in copies[:3]:
+        copy.wait()
     for z in range(NZ):
-        kinds = kind[z]
-        design = por[z]
-        collided = collide([pop[q, z] for q in range(Q)], design, kinds, speed)
+        collided = collide([pop[q, z] for q in range(Q)], por[z], kind[z], speed)
         for q in range(Q):
             moved[q, z] = collided[q]
-
-        def value(what, which):
-            if what == FORWARD:
-                return collided[which]
-            if what == ADJOINT:
-                return adj[which, z]
-            return design if what == DESIGN else kinds.astype(jnp.float32)
-
+    copies[3].wait()
+
+    def value(what, which, z):
+        if what == FORWARD:
+            return moved[which, z]
+        if what == ADJOINT:
+            return adj[which, z]
+        return por[z] if what == DESIGN else kind[z].astype(jnp.float32)
+
+    def write(up, down):
         for table, out in ((Z_UP_AT, up), (Z_DOWN_AT, down)):
-            for (what, which, plane), at in table.items():
-                if plane == z:
-                    out[at] = value(what, which)
-
-
-def rows_kernel(moved, adj, por, kind, below, above, shifted, up, down):
+            for entry, at in table.items():
+                out[at] = value(*entry)
+
+    by_side("gz", write, first, second)
+
+
+def copy_both(up, down, first, second):
+    for i in range(up.shape[0] // ROWS):
+        rows = pl.ds(i * ROWS, ROWS)
+        first[rows, :] = up[rows, :]
+        second[rows, :] = down[rows, :]
+
+
+def rows_kernel(moved, adj, por, kind, one, two, shifted, up, down, first, second):
+    below, above = from_side("gz", one, two)
+
     def plane_of(what, which, z):
         if z < 0:
-            return below[Z_UP_AT[what, which, z + NZ]]
+            return below(Z_UP_AT[what, which, z + NZ])
         if z >= NZ:
-            return above[Z_DOWN_AT[what, which, z - NZ]]
+            return above(Z_DOWN_AT[what, which, z - NZ])
         if what == FORWARD:
             return moved[which, z]
         if what == ADJOINT:
@@ -256,26 +305,33 @@
                     s = -VELOCITIES[q][2]
                 terms.append((sign, plane_of(what, q, t - 1 - s)))
             shifted[pl.ds((i * EXT + t) * ROWS, ROWS), :] = add_up(terms)
-    for table, out in ((Y_UP, up), (Y_DOWN, down)):
-        for at, (i, row) in enumerate(table):
-            out[pl.ds(at * EXT, EXT), :] = shifted[
-                pl.ds(i * EXT * ROWS + row, EXT, stride=ROWS), :
-            ]
-        used = len(table) * EXT
-        out[pl.ds(used, out.shape[0] - used), :] = jnp.zeros(
-            (out.shape[0] - used, NX), jnp.float32
-        )
-
-
-def columns_kernel(shifted, up, down, left, right, wide, packed):
+    def write(forward, backward):
+        for table, out in ((Y_UP, forward), (Y_DOWN, backward)):
+            for at, (i, row) in enumerate(table):
+                out[pl.ds(at * EXT, EXT), :] = shifted[
+                    pl.ds(i * EXT * ROWS + row, EXT, stride=ROWS), :
+                ]
+            used = len(table) * EXT
+            out[pl.ds(used, out.shape[0] - used), :] = jnp.zeros(
+                (out.shape[0] - used, NX), jnp.float32
+            )
+
+    write(up, down)
+    if "gy" in SWAPPED:
+        by_side("gy", functools.partial(copy_both, up, down), first, second)
+
+
+def columns_kernel(shifted, up, down, one, two, wide, packed):
+    left, right = from_side("gy", one, two)
     row = lax.broadcasted_iota(jnp.int32, (NY, NX), 0)
     lane = lax.broadcasted_iota(jnp.int32, (NY, NX), 1)
 
     def rows_of(ref, at):
-        return ref[pl.ds(at * EXT, ROWS), :]
+        rows = (pl.ds(at * EXT, ROWS), slice(None))
+        return ref(rows) if callable(ref) else ref[rows]
 
     def row_of(ref, at, t):
-        return jnp.broadcast_to(ref[pl.ds(at * EXT + t, 1), :], (NY, NX))
+        return jnp.broadcast_to(ref((pl.ds(at * EXT + t, 1), slice(None))), (NY, NX))
 
     def tile_of(entry, t):
         i = Y_AT[entry]
@@ -323,11 +379,12 @@
         packed[u] = total
 
 
-def adjoint_kernel(wide, packed, before, after, pop, por, kind, out, sense, states):
+def adjoint_kernel(wide, packed, one, two, pop, por, kind, out, sense, states):
     lane = lax.broadcasted_iota(jnp.int32, (NY, NX), 1)
     row = lax.broadcasted_iota(jnp.int32, (NY, NX), 0)
     slot = lane & 3
-    beside = [jnp.where(slot < 2, before[u], after[u]) for u in range(PACKED)]
+    before, after = from_side("gx", one, two)
+    beside = [jnp.where(slot < 2, before(u), after(u)) for u in range(PACKED)]
 
     def value(entry, t):
         f = X_AT[entry]
@@ -428,10 +485,14 @@
 
 VMEM = pl.BlockSpec(memory_space=pltpu.VMEM)
 SMEM = pl.BlockSpec(memory_space=pltpu.SMEM)
+HBM = pl.BlockSpec(memory_space=pltpu.HBM)
 
 
 def call(kernel, shapes, specs, scratch=()):
-    out = [jax.ShapeDtypeStruct(shape, jnp.float32) for shape in shapes]
+    out = [
+        shape if isinstance(shape, jax.ShapeDtypeStruct) else jax.ShapeDtypeStruct(shape, jnp.float32)
+        for shape in shapes
+    ]
     return pl.pallas_call(
         kernel,
         out_shape=out,
@@ -442,40 +503,58 @@
     )
 
 
-def both_ways(forward, backward, axis):
+def both_ways(first, second, axis):
     count = lax.axis_size(axis)
-    ahead = [(i, (i + 1) % count) for i in range(count)]
-    behind = [(t, s) for s, t in ahead]
-    return lax.ppermute(forward, axis, ahead), lax.ppermute(backward, axis, behind)
+    if axis in SWAPPED:
+        one = [(i, i ^ 1) for i in range(count)]
+        two = [((i + 1) % count, ((i ^ 1) + 1) % count) for i in range(count)]
+    else:
+        one = [(i, (i + 1) % count) for i in range(count)]
+        two = [(t, s) for s, t in one]
+    return lax.ppermute(first, axis, one), lax.ppermute(second, axis, two)
 
 
 def on_device(populations, porosity, node_type, step_index, adjoint_end):
     tile = (NY, NX)
-    moved, up, down = call(
+    moved, first, second, pop, adj, por, kind = call(
         collide_kernel,
-        [(Q, NZ, *tile), (len(Z_UP), *tile), (len(Z_DOWN), *tile)],
-        [SMEM] + [VMEM] * 4,
-    )(step_index, populations, adjoint_end, porosity, node_type)
-    below, above = both_ways(up, down, "gz")
-    shifted, up, down = call(
-        rows_kernel,
-        [(len(Y_FIELDS) * EXT * ROWS, NX), (Y_UP_ROWS, NX), (Y_DOWN_ROWS, NX)],
+        [(Q, NZ, *tile), (len(Z_UP), *tile), (len(Z_DOWN), *tile)]
+        + [(Q, NZ, *tile), (Q, NZ, *tile), (NZ, *tile), jax.ShapeDtypeStruct((NZ, *tile), jnp.int32)],
+        [SMEM] + [HBM] * 4,
+        [pltpu.SemaphoreType.DMA((4,))],
+    )(
+        step_index,
+        *(
+            pltpu.with_memory_space_constraint(x, pltpu.HBM)
+            for x in (populations, adjoint_end, porosity, node_type)
+        ),
+    )
+    one, two = both_ways(first, second, "gz")
+    shifted, up, down, *copies = call(
+        rows_kernel if "gy" in SWAPPED else functools.partial(without_copies, rows_kernel),
+        [(len(Y_FIELDS) * EXT * ROWS, NX), (Y_UP_ROWS, NX), (Y_DOWN_ROWS, NX)]
+        + [(Y_UP_ROWS, NX), (Y_DOWN_ROWS, NX)] * ("gy" in SWAPPED),
         [VMEM] * 6,
-    )(moved, adjoint_end, porosity, node_type, below, above)
-    left, right = both_ways(up, down, "gy")
+    )(moved, adj, por, kind, one, two)
+    first, second = copies or (up, down)
+    one, two = both_ways(first, second, "gy")
     wide, packed = call(
         columns_kernel,
         [(len(X_FIELDS) * (EXT + 2) * ROWS, NX), (PACKED, *tile)],
         [VMEM] * 5,
-    )(shifted, up, down, left, right)
-    before, after = both_ways(packed, packed, "gx")
+    )(shifted, up, down, one, two)
+    one, two = both_ways(packed, packed, "gx")
     adjoint, sense = call(
         adjoint_kernel,
         [(Q, NZ, *tile), (NZ, *tile)],
         [VMEM] * 7,
         [pltpu.VMEM((Q * (SIDES + 1) * ROWS, NX), jnp.float32)],
-    )(wide, packed, before, after, populations, porosity, node_type)
+    )(wide, packed, one, two, pop, por, kind)
     return adjoint, sense
+
+
+def without_copies(kernel, *refs):
+    kernel(*refs, None, None)
 
 
 def solution(mesh):

time: 45.5 us -> 41.3 us (0.908)
  the two profiles are of different devices: /device:TPU:14 before, /device:TPU:23 now
where the time goes in v3:
time: 41.3 us; the launch traced here: 41 us
  starting transfers between devices  27.2 us (66%)
  waiting for transfers between devices  9.44 us (23%)
  Pallas kernels  3.01 us (7%)
  between operations  1.35 us (3%)
    ppermute x6, starting transfers between devices, both_ways(): return (lax.ppermute(first, axis, one), lax.ppermute(second, axis, two))  27.2 us
    ppermute x6, waiting for transfers between devices, both_ways(): return (lax.ppermute(first, axis, one), lax.ppermute(second, axis, two))  9.44 us
    pallas_call x1, Pallas kernels, on_device(): call(adjoint_kernel, [(Q, NZ, *tile), (NZ, *tile)], [VMEM] * 7, [pltpu.VM...  1.36 us
    pallas_call x1, Pallas kernels, on_device(): call(collide_kernel, [(Q, NZ, *tile), (len(Z_UP), *tile), (len(Z_DOWN), *...  1.19 us
  transfers between devices with their start and end apart: 6, of which 5 were waited for; matrix products, arithmetic and copies ran while one was open for 0% of the time, Pallas kernels for 0%

profile of v3, /device:TPU:23, one launch (start us, length us, event | category | flops | bytes accessed | tf_op | source)
XLA Modules:
  0.0 41.0 jit_solution(7386479056684204431)
XLA Ops:
  1.3 1.2 %shard_map.68 = (f32[19,4,8,128]{3,2,1,0:T(8,128)S(1)}, f32[40,8,128]{2,1,0:T(8,128)S(1)}, f32[40,8,128]{2,1,0:T(8,128)S(1)}, f32[19,4,8,128]{3,2,1,0:T(8,128)S(...) custom-call(s32[1]{0:T(128)S(6)} %copy.7.step, f32[19,4,8,128]{3,2,1,0:T(8,128)} %pop_hbm.1, ...), custom_call_target="tpu_custom_call" | custom-call | tf_op jit(solution)/shard_map/pallas_call | solution.py:519
  2.5 4.0 %collective-permute-start = (f32[40,8,128]{2,1,0:T(8,128)S(1)}, f32[40,8,128]{2,1,0:T(8,128)S(1)}, u32[]{:S(2)}, u32[]{:S(2)}) collective-permute-start(f32[40,8,128]{2,1,0:T(8,128)S(1)} %get-tuple-element.18), channel_id=1, source_target_pairs={{0,1},{1,2},{2,3},{3,4},{4,5},{5,6},{6,7},{7,0},{8,9},{9,10},{10,1... | collective-permute-start | bytes 491528 | tf_op jit(solution)/shard_map/ppermute | solution.py:514
  6.5 8.6 %collective-permute-start.1 = (f32[40,8,128]{2,1,0:T(8,128)S(1)}, f32[40,8,128]{2,1,0:T(8,128)S(1)}, u32[]{:S(2)}, u32[]{:S(2)}) collective-permute-start(f32[40,8,128]{2,1,0:T(8,128)S(1)} %get-tuple-element.19), channel_id=1, source_target_pairs={{1,0},{2,1},{3,2},{4,3},{5,4},{6,5},{7,6},{0,7},{9,8},{10,9},{11,1... | collective-permute-start | bytes 491528 | tf_op jit(solution)/shard_map/ppermute | solution.py:514
  15.1 2.0 %collective-permute-done.refs_4_ = f32[40,8,128]{2,1,0:T(8,128)S(1)} collective-permute-done((f32[40,8,128]{2,1,0:T(8,128)S(1)}, f32[40,8,128]{2,1,0:T(8,128)S(1)}, u32[]{:S(2)}, u32[]{:S(2)}) %collective-permute-start) | collective-permute-done | bytes 163872 | tf_op jit(solution)/shard_map/ppermute | solution.py:514
  17.1 0.9 %collective-permute-done.1.refs_5_ = f32[40,8,128]{2,1,0:T(8,128)S(1)} collective-permute-done((f32[40,8,128]{2,1,0:T(8,128)S(1)}, f32[40,8,128]{2,1,0:T(8,128)S(1)}, u32[]{:S(2)}, u32[]{:S(2)}) %collective-permute-start.1) | collective-permute-done | bytes 163872 | tf_op jit(solution)/shard_map/ppermute | solution.py:514
  17.9 0.1 shard_map.69
  18.0 3.1 %collective-permute-start.2 = (f32[216,128]{1,0:T(8,128)S(1)}, f32[216,128]{1,0:T(8,128)S(1)}, u32[]{:S(2)}, u32[]{:S(2)}) collective-permute-start(f32[216,128]{1,0:T(8,128)S(1)} %get-tuple-element.21.up), channel_id=1, source_target_pairs={{0,8},{8,16},{16,24},{24,32},{32,40},{40,48},{48,56},{56,0},{1,9},... | collective-permute-start | bytes 331784 | tf_op jit(solution)/shard_map/ppermute | solution.py:514
  21.2 2.2 %collective-permute-start.3 = (f32[216,128]{1,0:T(8,128)S(1)}, f32[216,128]{1,0:T(8,128)S(1)}, u32[]{:S(2)}, u32[]{:S(2)}) collective-permute-start(f32[216,128]{1,0:T(8,128)S(1)} %get-tuple-element.22.down), channel_id=1, source_target_pairs={{8,0},{16,8},{24,16},{32,24},{40,32},{48,40},{56,48},{0,56},{9,1},... | collective-permute-start | bytes 331784 | tf_op jit(solution)/shard_map/ppermute | solution.py:514
  23.3 0.2 collective-permute-done.2.one
  23.5 5.2 %collective-permute-done.3.two = f32[216,128]{1,0:T(8,128)S(1)} collective-permute-done((f32[216,128]{1,0:T(8,128)S(1)}, f32[216,128]{1,0:T(8,128)S(1)}, u32[]{:S(2)}, u32[]{:S(2)}) %collective-permute-start.3) | collective-permute-done | bytes 110624 | tf_op jit(solution)/shard_map/ppermute | solution.py:514
  28.8 0.3 shard_map.70
  29.1 7.4 %collective-permute-start.5 = (f32[8,8,128]{2,1,0:T(8,128)S(1)}, f32[8,8,128]{2,1,0:T(8,128)S(1)}, u32[]{:S(2)}, u32[]{:S(2)}) collective-permute-start(f32[8,8,128]{2,1,0:T(8,128)S(1)} %get-tuple-element.24.packed), channel_id=1, source_target_pairs={{64,128},{128,64},{192,256},{256,192},{320,384},{384,320},{448,0},... | collective-permute-start | bytes 98312 | tf_op jit(solution)/shard_map/ppermute | solution.py:514
  36.5 1.9 %collective-permute-start.4 = (f32[8,8,128]{2,1,0:T(8,128)S(1)}, f32[8,8,128]{2,1,0:T(8,128)S(1)}, u32[]{:S(2)}, u32[]{:S(2)}) collective-permute-start(f32[8,8,128]{2,1,0:T(8,128)S(1)} %get-tuple-element.24.packed), channel_id=1, source_target_pairs={{0,64},{64,0},{128,192},{192,128},{256,320},{320,256},{384,448},{4... | collective-permute-start | bytes 98312 | tf_op jit(solution)/shard_map/ppermute | solution.py:514
  38.5 0.0 collective-permute-done.5.two
  38.5 1.2 %collective-permute-done.4.one = f32[8,8,128]{2,1,0:T(8,128)S(1)} collective-permute-done((f32[8,8,128]{2,1,0:T(8,128)S(1)}, f32[8,8,128]{2,1,0:T(8,128)S(1)}, u32[]{:S(2)}, u32[]{:S(2)}) %collective-permute-start.4) | collective-permute-done | bytes 32800 | tf_op jit(solution)/shard_map/ppermute | solution.py:514
  39.6 1.4 %shard_map.71 = (f32[19,4,8,128]{3,2,1,0:T(8,128)}, f32[4,8,128]{2,1,0:T(8,128)}) custom-call(f32[1920,128]{1,0:T(8,128)S(1)} %get-tuple-element.23.wide, f32[8,8,128]{2,1,0:T(8,128)S(1)} %get-tuple-element.24.packed, f32[8,8,128]{2,1,0:T(8,128)S(1)} %collective-permute-done.4.one, f32[8,8,128]{2,1,0:T(8,128)S(1)} %collective-permute-done.5.two, ...), custom_call_target="tpu_custom_call" | custom-call | tf_op jit(solution)/shard_map/pallas_call | solution.py:547
Async XLA Ops:
  2.5 14.6 %collective-permute-start = (f32[40,8,128]{2,1,0:T(8,128)S(1)}, f32[40,8,128]{2,1,0:T(8,128)S(1)}, u32[]{:S(2)}, u32[]{:S(2)}) collective-permute-start(f32[40,8,128]{2,1,0:T(8,128)S(1)} %get-tuple-element.18), channel_id=1, source_target_pairs={{0,1},{1,2},{2,3},{3,4},{4,5},{5,6},{6,7},{7,0},{8,9},{9,10},{10,1... | collective-permute-start | bytes 491528 | tf_op jit(solution)/shard_map/ppermute | solution.py:514
  6.5 11.4 %collective-permute-start.1 = (f32[40,8,128]{2,1,0:T(8,128)S(1)}, f32[40,8,128]{2,1,0:T(8,128)S(1)}, u32[]{:S(2)}, u32[]{:S(2)}) collective-permute-start(f32[40,8,128]{2,1,0:T(8,128)S(1)} %get-tuple-element.19), channel_id=1, source_target_pairs={{1,0},{2,1},{3,2},{4,3},{5,4},{6,5},{7,6},{0,7},{9,8},{10,9},{11,1... | collective-permute-start | bytes 491528 | tf_op jit(solution)/shard_map/ppermute | solution.py:514
  18.0 5.5 %collective-permute-start.2 = (f32[216,128]{1,0:T(8,128)S(1)}, f32[216,128]{1,0:T(8,128)S(1)}, u32[]{:S(2)}, u32[]{:S(2)}) collective-permute-start(f32[216,128]{1,0:T(8,128)S(1)} %get-tuple-element.21.up), channel_id=1, source_target_pairs={{0,8},{8,16},{16,24},{24,32},{32,40},{40,48},{48,56},{56,0},{1,9},... | collective-permute-start | bytes 331784 | tf_op jit(solution)/shard_map/ppermute | solution.py:514
  21.2 7.6 %collective-permute-start.3 = (f32[216,128]{1,0:T(8,128)S(1)}, f32[216,128]{1,0:T(8,128)S(1)}, u32[]{:S(2)}, u32[]{:S(2)}) collective-permute-start(f32[216,128]{1,0:T(8,128)S(1)} %get-tuple-element.22.down), channel_id=1, source_target_pairs={{8,0},{16,8},{24,16},{32,24},{40,32},{48,40},{56,48},{0,56},{9,1},... | collective-permute-start | bytes 331784 | tf_op jit(solution)/shard_map/ppermute | solution.py:514
  29.1 9.3 %collective-permute-start.5 = (f32[8,8,128]{2,1,0:T(8,128)S(1)}, f32[8,8,128]{2,1,0:T(8,128)S(1)}, u32[]{:S(2)}, u32[]{:S(2)}) collective-permute-start(f32[8,8,128]{2,1,0:T(8,128)S(1)} %get-tuple-element.24.packed), channel_id=1, source_target_pairs={{64,128},{128,64},{192,256},{256,192},{320,384},{384,320},{448,0},... | collective-permute-start | bytes 98312 | tf_op jit(solution)/shard_map/ppermute | solution.py:514
  36.5 3.1 %collective-permute-start.4 = (f32[8,8,128]{2,1,0:T(8,128)S(1)}, f32[8,8,128]{2,1,0:T(8,128)S(1)}, u32[]{:S(2)}, u32[]{:S(2)}) collective-permute-start(f32[8,8,128]{2,1,0:T(8,128)S(1)} %get-tuple-element.24.packed), channel_id=1, source_target_pairs={{0,64},{64,0},{128,192},{192,128},{256,320},{320,256},{384,448},{4... | collective-permute-start | bytes 98312 | tf_op jit(solution)/shard_map/ppermute | solution.py:514

commit v4 on v3

--- a/solution.py
+++ b/solution.py
@@ -40,6 +40,9 @@
 SIDES = EXT + 2
 ROWS = 8
 SWAPPED = ("gx",)
+REVERSED = ("gz",)
+
+FLUID, WALL, INLET, OUTLET = -1, 0, 1, 2
 
 FORWARD, ADJOINT, DESIGN, KIND = range(4)
 
@@ -132,9 +135,9 @@
 def collide(f, porosity, kinds, speed):
     density, flow = moments(f)
     inverse = 1.0 / density
-    fluid = kinds == 0
-    wall = kinds == 1
-    inlet = kinds == 2
+    fluid = kinds == FLUID
+    wall = kinds == WALL
+    inlet = kinds == INLET
     damping = RAMP * (1.0 - porosity) / (RAMP + porosity)
     kept = jnp.where(fluid, 1.0 - damping, 1.0)
     v = [
@@ -154,14 +157,17 @@
     return out
 
 
-def pull_back(density, flow, h, porosity, kinds, wanted):
-    fluid = kinds == 0
-    wall = kinds == 1
-    outlet = kinds == 3
+def prepare(density, flow, porosity, kinds):
     inverse = 1.0 / density
-    u = [flow[i] * inverse for i in range(3)]
+    return [density, *(flow[i] * inverse for i in range(3)), 1.0 / (RAMP + porosity)]
+
+
+def pull_back(state, h, porosity, kinds, wanted):
+    density, *u, ramp = state
+    fluid = kinds == FLUID
+    wall = kinds == WALL
+    outlet = kinds == OUTLET
     square = u[0] * u[0] + u[1] * u[1] + u[2] * u[2]
-    ramp = 1.0 / (RAMP + porosity)
     damping = jnp.where(fluid, RAMP * (1.0 - porosity) * ramp, 0.0)
     kept = 1.0 - damping
     v = [kept * u[i] for i in range(3)]
@@ -215,6 +221,8 @@
 
 
 def by_side(axis, act, first, second):
+    if axis in REVERSED:
+        first, second = second, first
     if axis not in SWAPPED:
         act(first, second)
         return
@@ -230,6 +238,8 @@
 
 
 def from_side(axis, first, second):
+    if axis in REVERSED:
+        first, second = second, first
     if axis not in SWAPPED:
         return (lambda at: first[at]), (lambda at: second[at])
     even = lax.rem(lax.axis_index(axis), 2) == 0
@@ -240,12 +250,12 @@
 
 
 def collide_kernel(
-    step, pop_hbm, adj_hbm, por_hbm, kind_hbm, moved, first, second, pop, adj, por, kind, done
+    step, pop_hbm, adj_hbm, por_hbm, kind_hbm, moved, first, second, pop, adj, por, kind, raw, done
 ):
     copies = [
         pltpu.make_async_copy(source, target, done.at[i])
         for i, (source, target) in enumerate(
-            ((pop_hbm, pop), (por_hbm, por), (kind_hbm, kind), (adj_hbm, adj))
+            ((pop_hbm, pop), (por_hbm, por), (kind_hbm, raw), (adj_hbm, adj))
         )
     ]
     for copy in copies:
@@ -255,6 +265,7 @@
     for copy in copies[:3]:
         copy.wait()
     for z in range(NZ):
+        kind[z] = (raw[z] - 1).astype(jnp.float32)
         collided = collide([pop[q, z] for q in range(Q)], por[z], kind[z], speed)
         for q in range(Q):
             moved[q, z] = collided[q]
@@ -265,7 +276,7 @@
             return moved[which, z]
         if what == ADJOINT:
             return adj[which, z]
-        return por[z] if what == DESIGN else kind[z].astype(jnp.float32)
+        return por[z] if what == DESIGN else kind[z]
 
     def write(up, down):
         for table, out in ((Z_UP_AT, up), (Z_DOWN_AT, down)):
@@ -294,7 +305,7 @@
             return moved[which, z]
         if what == ADJOINT:
             return adj[which, z]
-        return por[z] if what == DESIGN else kind[z].astype(jnp.float32)
+        return por[z] if what == DESIGN else kind[z]
 
     for i, (what, _, parts, _) in enumerate(Y_FIELDS):
         for t in range(EXT):
@@ -379,108 +390,128 @@
         packed[u] = total
 
 
-def adjoint_kernel(wide, packed, one, two, pop, por, kind, out, sense, states):
-    lane = lax.broadcasted_iota(jnp.int32, (NY, NX), 1)
-    row = lax.broadcasted_iota(jnp.int32, (NY, NX), 0)
-    slot = lane & 3
-    before, after = from_side("gx", one, two)
-    beside = [jnp.where(slot < 2, before(u), after(u)) for u in range(PACKED)]
-
-    def value(entry, t):
-        f = X_AT[entry]
-        u, j = f // PER_TILE, f % PER_TILE
-        s = shift_of(entry)
-        if t == SIDES:
-            if s > 0:
-                base = jnp.where(slot == 1, pltpu.roll(beside[u], 1, 1), pltpu.roll(packed[u], 1, 1))
-            elif s < 0:
-                base = jnp.where(
-                    slot == 2, pltpu.roll(beside[u], NX - 1, 1), pltpu.roll(packed[u], NX - 1, 1)
-                )
-            else:
-                base = beside[u]
-            return pltpu.roll(base, NX - 32 * j, 1) if j else base
-        own = wide[pl.ds((f * (EXT + 2) + t) * ROWS, ROWS), :]
-        k = j * (EXT + 2) + t
-        if s > 0:
-            return jnp.where(
-                lane == 0, pltpu.roll(beside[u], NX - (4 * k + 1), 1), pltpu.roll(own, 1, 1)
-            )
-        if s < 0:
-            return jnp.where(
-                lane == NX - 1,
-                pltpu.roll(beside[u], (NX - 1 - (4 * k + 2)) % NX, 1),
-                pltpu.roll(own, NX - 1, 1),
-            )
-        return own
-
-    def at(q, t):
-        return pl.ds((q * (SIDES + 1) + t) * ROWS, ROWS)
-
-    for t in (SIDES, LOW, HIGH, 0, EXT - 1, *range(1, NZ + 1)):
-        if t == SIDES:
-            wanted = [q for q in range(Q) if VELOCITIES[q][0]]
-        elif t in (LOW, HIGH):
-            wanted = [q for q in range(Q) if VELOCITIES[q][1] == (1 if t == HIGH else -1)]
-        elif t in (0, EXT - 1):
-            wanted = [q for q in range(Q) if VELOCITIES[q][2] == (1 if t else -1)]
-        else:
-            wanted = range(Q)
-        parts = {s: [value((FORWARD, (s, i)), t) for i in range(3)] for s in (-1, 0, 1)}
-        density = parts[0][0] + parts[1][0] + parts[-1][0]
-        flow = [
-            parts[1][0] - parts[-1][0],
-            parts[0][1] + parts[1][1] + parts[-1][1],
-            parts[0][2] + parts[1][2] + parts[-1][2],
-        ]
-        h = [value((ADJOINT, q), t) for q in range(Q)]
-        back, by_porosity = pull_back(
-            density, flow, h, value((DESIGN, 0), t), value((KIND, 0), t), wanted
-        )
-        for q in wanted:
+STATE = 5
+
+
+def wanted_at(t):
+    if t == SIDES:
+        return list(range(Q))
+    if t in (LOW, HIGH):
+        return [q for q in range(Q) if VELOCITIES[q][1] == (1 if t == HIGH else -1)]
+    if t in (0, EXT - 1):
+        return [q for q in range(Q) if VELOCITIES[q][2] == (1 if t else -1)]
+    return list(range(Q))
+
+
+def later_adjoint(value):
+    parts = {s: [value((FORWARD, (s, i))) for i in range(3)] for s in (-1, 0, 1)}
+    density = parts[0][0] + parts[1][0] + parts[-1][0]
+    flow = [
+        parts[1][0] - parts[-1][0],
+        parts[0][1] + parts[1][1] + parts[-1][1],
+        parts[0][2] + parts[1][2] + parts[-1][2],
+    ]
+    h = [value((ADJOINT, q)) for q in range(Q)]
+    design, kinds = value((DESIGN, 0)), value((KIND, 0))
+    return prepare(density, flow, design, kinds), h, design, kinds
+
+
+def at(q, t):
+    return pl.ds((q * (SIDES + 1) + t) * ROWS, ROWS)
+
+
+def inner_kernel(wide, pop, por, kind, states, sense, ready):
+    for t in range(SIDES):
+
+        def value(entry, t=t):
+            own = wide[pl.ds((X_AT[entry] * (EXT + 2) + t) * ROWS, ROWS), :]
+            s = shift_of(entry)
+            return pltpu.roll(own, s % NX, 1) if s else own
+
+        back, by_porosity = pull_back(*later_adjoint(value), wanted_at(t))
+        for q in wanted_at(t):
             states[at(q, t), :] = back[q]
         if 1 <= t <= NZ:
             sense[t - 1] = by_porosity
+    for z in range(NZ):
+        density, flow = moments([pop[q, z] for q in range(Q)])
+        for i, part in enumerate(prepare(density, flow, por[z], kind[z])):
+            ready[i, z] = part
+
+
+def adjoint_kernel(states, sense, ready, packed, one, two, por, kind, out_hbm, sense_hbm, out, sum_, sides, done):
+    lane = lax.broadcasted_iota(jnp.int32, (NY, NX), 1)
+    row = lax.broadcasted_iota(jnp.int32, (NY, NX), 0)
+    before, after = from_side("gx", one, two)
+    slot = lane & 3
+    ends = []
+    for u in range(PACKED):
+        s = shift_of(X_FIELDS[u * PER_TILE])
+        own = packed[u]
+        if s > 0:
+            ends.append(jnp.where(slot < 2, own, pltpu.roll(before(u), 2, 1)))
+        elif s < 0:
+            ends.append(jnp.where(slot < 2, pltpu.roll(after(u), NX - 2, 1), own))
+        else:
+            here = jnp.where(slot == 1, own, after(u))
+            there = jnp.where(slot == 1, before(u), own)
+            ends.append(
+                jnp.where(slot < 2, pltpu.roll(here, NX - 1, 1), pltpu.roll(there, 1, 1))
+            )
+
+    def value(entry):
+        u, j = divmod(X_AT[entry], PER_TILE)
+        return pltpu.roll(ends[u], NX - 32 * j, 1) if j else ends[u]
+
+    def together(tile):
+        return jnp.where(slot == 0, tile, pltpu.roll(tile, NX - 2, 1))
+
+    back, by_porosity = pull_back(*later_adjoint(value), wanted_at(SIDES))
+    for q in range(Q):
+        sides[q] = back[q] if VELOCITIES[q][0] else together(back[q])
+    by_porosity = together(by_porosity)
+    last, first_two, last_two = lane == NX - 1, lane < 2, lane >= NX - 2
+    outer = (lane == 0) | last
 
     def moved_x(q, t):
         tile = states[at(q, t), :]
         cx = VELOCITIES[q][0]
         if cx > 0:
-            return jnp.where(
-                lane == NX - 1,
-                pltpu.roll(states[at(q, SIDES), :], (NX - 1 - (4 * t + 2)) % NX, 1),
-                pltpu.roll(tile, NX - 1, 1),
-            )
+            turned = pltpu.roll(sides[q], NX - 2 - 4 * t, 1)
+            return jnp.where(last_two, turned, pltpu.roll(tile, NX - 1, 1))
         if cx < 0:
-            return jnp.where(
-                lane == 0,
-                pltpu.roll(states[at(q, SIDES), :], NX - (4 * t + 1), 1),
-                pltpu.roll(tile, 1, 1),
-            )
-        return tile
-
+            turned = pltpu.roll(sides[q], NX - 2 - 4 * t, 1)
+            return jnp.where(first_two, turned, pltpu.roll(tile, 1, 1))
+        return jnp.where(outer, pltpu.roll(sides[q], NX - 1 - 4 * t, 1), tile)
+
+    copies = []
     for z in range(NZ):
         h = []
         for q in range(Q):
             _, cy, cz = VELOCITIES[q]
             t = z + cz + 1
             tile = moved_x(q, t)
-            if cy > 0:
-                edge = moved_x(q, HIGH)[t : t + 1]
+            if cy:
+                edge = moved_x(q, HIGH if cy > 0 else LOW)[t : t + 1]
                 tile = jnp.where(
-                    row == NY - 1, jnp.broadcast_to(edge, (NY, NX)), pltpu.roll(tile, NY - 1, 0)
+                    row == (NY - 1 if cy > 0 else 0),
+                    jnp.broadcast_to(edge, (NY, NX)),
+                    pltpu.roll(tile, NY - 1 if cy > 0 else 1, 0),
                 )
-            elif cy < 0:
-                edge = moved_x(q, LOW)[t : t + 1]
-                tile = jnp.where(row == 0, jnp.broadcast_to(edge, (NY, NX)), pltpu.roll(tile, 1, 0))
             h.append(tile)
-        density, flow = moments([pop[q, z] for q in range(Q)])
-        back, by_porosity = pull_back(
-            density, flow, h, por[z], kind[z].astype(jnp.float32), range(Q)
+        back, now = pull_back(
+            [ready[i, z] for i in range(STATE)], h, por[z], kind[z], range(Q)
         )
         for q in range(Q):
-            out[q, z] = back[q]
-        sense[z] = sense[z] + by_porosity
+            out[z, q] = back[q]
+        copies.append(pltpu.make_async_copy(out.at[z], out_hbm.at[:, z], done.at[z]))
+        copies[-1].start()
+        then = jnp.where(outer, pltpu.roll(by_porosity, NX - 1 - 4 * (z + 1), 1), sense[z])
+        sum_[z] = then + now
+    copies.append(pltpu.make_async_copy(sum_, sense_hbm, done.at[NZ]))
+    copies[-1].start()
+    for copy in copies:
+        copy.wait()
 
 
 VMEM = pl.BlockSpec(memory_space=pltpu.VMEM)
@@ -488,7 +519,7 @@
 HBM = pl.BlockSpec(memory_space=pltpu.HBM)
 
 
-def call(kernel, shapes, specs, scratch=()):
+def call(kernel, shapes, specs, scratch=(), out_specs=None, cost=None):
     out = [
         shape if isinstance(shape, jax.ShapeDtypeStruct) else jax.ShapeDtypeStruct(shape, jnp.float32)
         for shape in shapes
@@ -497,8 +528,9 @@
         kernel,
         out_shape=out,
         in_specs=specs,
-        out_specs=[VMEM] * len(out),
+        out_specs=out_specs or [VMEM] * len(out),
         scratch_shapes=list(scratch),
+        cost_estimate=cost,
         compiler_params=pltpu.CompilerParams(vmem_limit_bytes=12 * 1024 * 1024),
     )
 
@@ -509,8 +541,12 @@
         one = [(i, i ^ 1) for i in range(count)]
         two = [((i + 1) % count, ((i ^ 1) + 1) % count) for i in range(count)]
     else:
-        one = [(i, (i + 1) % count) for i in range(count)]
+        one = [(i, i + 1) for i in range(count - 1)]
         two = [(t, s) for s, t in one]
+    if axis != "gx":
+        two = [(s, t) for s, t in two if abs(s - t) == 1]
+    if axis in REVERSED:
+        one, two = two, one
     return lax.ppermute(first, axis, one), lax.ppermute(second, axis, two)
 
 
@@ -519,9 +555,9 @@
     moved, first, second, pop, adj, por, kind = call(
         collide_kernel,
         [(Q, NZ, *tile), (len(Z_UP), *tile), (len(Z_DOWN), *tile)]
-        + [(Q, NZ, *tile), (Q, NZ, *tile), (NZ, *tile), jax.ShapeDtypeStruct((NZ, *tile), jnp.int32)],
+        + [(Q, NZ, *tile), (Q, NZ, *tile), (NZ, *tile), (NZ, *tile)],
         [SMEM] + [HBM] * 4,
-        [pltpu.SemaphoreType.DMA((4,))],
+        [pltpu.VMEM((NZ, *tile), jnp.int32), pltpu.SemaphoreType.DMA((4,))],
     )(
         step_index,
         *(
@@ -537,6 +573,8 @@
         [VMEM] * 6,
     )(moved, adj, por, kind, one, two)
     first, second = copies or (up, down)
+    if "gy" in REVERSED and not copies:
+        first, second = down, up
     one, two = both_ways(first, second, "gy")
     wide, packed = call(
         columns_kernel,
@@ -544,12 +582,24 @@
         [VMEM] * 5,
     )(shifted, up, down, one, two)
     one, two = both_ways(packed, packed, "gx")
+    states, part, ready = call(
+        inner_kernel,
+        [(Q * (SIDES + 1) * ROWS, NX), (NZ, *tile), (STATE, NZ, *tile)],
+        [VMEM] * 4,
+        cost=pl.CostEstimate(flops=20_000_000, bytes_accessed=4_000_000, transcendentals=0),
+    )(wide, pop, por, kind)
     adjoint, sense = call(
         adjoint_kernel,
         [(Q, NZ, *tile), (NZ, *tile)],
-        [VMEM] * 7,
-        [pltpu.VMEM((Q * (SIDES + 1) * ROWS, NX), jnp.float32)],
-    )(wide, packed, one, two, pop, por, kind)
+        [VMEM] * 8,
+        [
+            pltpu.VMEM((NZ, Q, *tile), jnp.float32),
+            pltpu.VMEM((NZ, *tile), jnp.float32),
+            pltpu.VMEM((Q, *tile), jnp.float32),
+            pltpu.SemaphoreType.DMA((NZ + 1,)),
+        ],
+        out_specs=[HBM] * 2,
+    )(states, part, ready, packed, one, two, por, kind)
     return adjoint, sense
 
 

time: 41.3 us -> 35.8 us (0.87)
  the two profiles are of different devices: /device:TPU:23 before, /device:TPU:279 now
where the time goes in v4:
time: 35.8 us; the launch traced here: 35.5 us
  starting transfers between devices  19.9 us (56%)
  waiting for transfers between devices  11 us (31%)
  Pallas kernels  3.24 us (9%)
  between operations  1.36 us (4%)
    ppermute x6, starting transfers between devices, both_ways(): return (lax.ppermute(first, axis, one), lax.ppermute(second, axis, two))  19.9 us
    ppermute x6, waiting for transfers between devices, both_ways(): return (lax.ppermute(first, axis, one), lax.ppermute(second, axis, two))  11 us
    pallas_call x1, Pallas kernels, on_device(): call(adjoint_kernel, [(Q, NZ, *tile), (NZ, *tile)], [VMEM] * 8, [pltpu.VM...  1.24 us
    pallas_call x1, Pallas kernels, on_device(): call(collide_kernel, [(Q, NZ, *tile), (len(Z_UP), *tile), (len(Z_DOWN), *...  1.19 us
  transfers between devices with their start and end apart: 6, of which 5 were waited for; matrix products, arithmetic and copies ran while one was open for 0% of the time, Pallas kernels for 1%

profile of v4, /device:TPU:279, one launch (start us, length us, event | category | flops | bytes accessed | tf_op | source)
XLA Modules:
  0.0 35.5 jit_solution(17216125122785745463)
XLA Ops:
  1.3 1.2 %shard_map.68 = (f32[19,4,8,128]{3,2,1,0:T(8,128)S(1)}, f32[40,8,128]{2,1,0:T(8,128)S(1)}, f32[40,8,128]{2,1,0:T(8,128)S(1)}, f32[19,4,8,128]{3,2,1,0:T(8,128)S(...) custom-call(s32[1]{0:T(128)S(6)} %copy.7.step, f32[19,4,8,128]{3,2,1,0:T(8,128)} %pop_hbm.1, ...), custom_call_target="tpu_custom_call" | custom-call | tf_op jit(solution)/shard_map/pallas_call | solution.py:555
  2.5 1.9 %collective-permute-start = (f32[40,8,128]{2,1,0:T(8,128)S(1)}, f32[40,8,128]{2,1,0:T(8,128)S(1)}, u32[]{:S(2)}, u32[]{:S(2)}) collective-permute-start(f32[40,8,128]{2,1,0:T(8,128)S(1)} %get-tuple-element.21), channel_id=1, source_target_pairs={{1,0},{2,1},{3,2},{4,3},{5,4},{6,5},{7,6},{9,8},{10,9},{11,10},{12... | collective-permute-start | bytes 491528 | tf_op jit(solution)/shard_map/ppermute | solution.py:550
  4.4 3.4 %collective-permute-start.1 = (f32[40,8,128]{2,1,0:T(8,128)S(1)}, f32[40,8,128]{2,1,0:T(8,128)S(1)}, u32[]{:S(2)}, u32[]{:S(2)}) collective-permute-start(f32[40,8,128]{2,1,0:T(8,128)S(1)} %get-tuple-element.22), channel_id=1, source_target_pairs={{0,1},{1,2},{2,3},{3,4},{4,5},{5,6},{6,7},{8,9},{9,10},{10,11},{11... | collective-permute-start | bytes 491528 | tf_op jit(solution)/shard_map/ppermute | solution.py:550
  7.8 1.7 %collective-permute-done.refs_4_ = f32[40,8,128]{2,1,0:T(8,128)S(1)} collective-permute-done((f32[40,8,128]{2,1,0:T(8,128)S(1)}, f32[40,8,128]{2,1,0:T(8,128)S(1)}, u32[]{:S(2)}, u32[]{:S(2)}) %collective-permute-start) | collective-permute-done | bytes 163872 | tf_op jit(solution)/shard_map/ppermute | solution.py:550
  9.4 3.1 %collective-permute-done.1.refs_5_ = f32[40,8,128]{2,1,0:T(8,128)S(1)} collective-permute-done((f32[40,8,128]{2,1,0:T(8,128)S(1)}, f32[40,8,128]{2,1,0:T(8,128)S(1)}, u32[]{:S(2)}, u32[]{:S(2)}) %collective-permute-start.1) | collective-permute-done | bytes 163872 | tf_op jit(solution)/shard_map/ppermute | solution.py:550
  12.6 0.1 shard_map.69
  12.7 3.1 %collective-permute-start.2 = (f32[216,128]{1,0:T(8,128)S(1)}, f32[216,128]{1,0:T(8,128)S(1)}, u32[]{:S(2)}, u32[]{:S(2)}) collective-permute-start(f32[216,128]{1,0:T(8,128)S(1)} %get-tuple-element.24.up), channel_id=1, source_target_pairs={{0,8},{8,16},{16,24},{24,32},{32,40},{40,48},{48,56},{1,9},{9,17},... | collective-permute-start | bytes 331784 | tf_op jit(solution)/shard_map/ppermute | solution.py:550
  15.8 2.2 %collective-permute-start.3 = (f32[216,128]{1,0:T(8,128)S(1)}, f32[216,128]{1,0:T(8,128)S(1)}, u32[]{:S(2)}, u32[]{:S(2)}) collective-permute-start(f32[216,128]{1,0:T(8,128)S(1)} %get-tuple-element.25.down), channel_id=1, source_target_pairs={{8,0},{16,8},{24,16},{32,24},{40,32},{48,40},{56,48},{9,1},{17,9},... | collective-permute-start | bytes 331784 | tf_op jit(solution)/shard_map/ppermute | solution.py:550
  18.0 0.2 collective-permute-done.2.one
  18.2 5.2 %collective-permute-done.3.two = f32[216,128]{1,0:T(8,128)S(1)} collective-permute-done((f32[216,128]{1,0:T(8,128)S(1)}, f32[216,128]{1,0:T(8,128)S(1)}, u32[]{:S(2)}, u32[]{:S(2)}) %collective-permute-start.3) | collective-permute-done | bytes 110624 | tf_op jit(solution)/shard_map/ppermute | solution.py:550
  23.4 0.3 shard_map.70
  23.8 7.4 %collective-permute-start.5 = (f32[8,8,128]{2,1,0:T(8,128)S(1)}, f32[8,8,128]{2,1,0:T(8,128)S(1)}, u32[]{:S(2)}, u32[]{:S(2)}) collective-permute-start(f32[8,8,128]{2,1,0:T(8,128)S(1)} %get-tuple-element.31.packed), channel_id=1, source_target_pairs={{64,128},{128,64},{192,256},{256,192},{320,384},{384,320},{448,0},... | collective-permute-start | bytes 98312 | tf_op jit(solution)/shard_map/ppermute | solution.py:550
  31.2 1.9 %collective-permute-start.4 = (f32[8,8,128]{2,1,0:T(8,128)S(1)}, f32[8,8,128]{2,1,0:T(8,128)S(1)}, u32[]{:S(2)}, u32[]{:S(2)}) collective-permute-start(f32[8,8,128]{2,1,0:T(8,128)S(1)} %get-tuple-element.31.packed), channel_id=1, source_target_pairs={{0,64},{64,0},{128,192},{192,128},{256,320},{320,256},{384,448},{4... | collective-permute-start | bytes 98312 | tf_op jit(solution)/shard_map/ppermute | solution.py:550
  33.1 0.4 %shard_map.71 = (f32[1368,128]{1,0:T(8,128)S(1)}, f32[4,8,128]{2,1,0:T(8,128)S(1)}, f32[5,4,8,128]{3,2,1,0:T(8,128)S(1)}) custom-call(f32[1920,128]{1,0:T(8,128)S(1)} %get-tuple-element.26.wide, f32[19,4,8,128]{3,2,1,0:T(8,128)S(1)} %get-tuple-element.27.pop, f32[4,8,128]{2,1,0:T(8,128)S(1)} %get-tuple-element.19.refs_2_.por, ...), custom_call_target="tpu_custom_call" | custom-call | flops 20000000 | bytes 4000000 | tf_op jit(solution)/shard_map/pallas_call | solution.py:585
  33.5 0.0 collective-permute-done.5.two
  33.5 0.8 %collective-permute-done.4.one = f32[8,8,128]{2,1,0:T(8,128)S(1)} collective-permute-done((f32[8,8,128]{2,1,0:T(8,128)S(1)}, f32[8,8,128]{2,1,0:T(8,128)S(1)}, u32[]{:S(2)}, u32[]{:S(2)}) %collective-permute-start.4) | collective-permute-done | bytes 32800 | tf_op jit(solution)/shard_map/ppermute | solution.py:550
  34.3 1.2 %shard_map.72 = (f32[19,4,8,128]{3,2,1,0:T(8,128)}, f32[4,8,128]{2,1,0:T(8,128)}) custom-call(f32[1368,128]{1,0:T(8,128)S(1)} %get-tuple-element.28.states, f32[4,8,128]{2,1,0:T(8,128)S(1)} %get-tuple-element.29.sense, f32[5,4,8,128]{3,2,1,0:T(8,128)S(1)} %get-tuple-element.30.ready, f32[8,8,128]{2,1,0:T(8,128)S(1)} %get-tuple-element.31.packed, ...), custom_call_target="tpu_custom_call" | custom-call | tf_op jit(solution)/shard_map/pallas_call | solution.py:591
Async XLA Ops:
  2.5 7.0 %collective-permute-start = (f32[40,8,128]{2,1,0:T(8,128)S(1)}, f32[40,8,128]{2,1,0:T(8,128)S(1)}, u32[]{:S(2)}, u32[]{:S(2)}) collective-permute-start(f32[40,8,128]{2,1,0:T(8,128)S(1)} %get-tuple-element.21), channel_id=1, source_target_pairs={{1,0},{2,1},{3,2},{4,3},{5,4},{6,5},{7,6},{9,8},{10,9},{11,10},{12... | collective-permute-start | bytes 491528 | tf_op jit(solution)/shard_map/ppermute | solution.py:550
  4.4 8.2 %collective-permute-start.1 = (f32[40,8,128]{2,1,0:T(8,128)S(1)}, f32[40,8,128]{2,1,0:T(8,128)S(1)}, u32[]{:S(2)}, u32[]{:S(2)}) collective-permute-start(f32[40,8,128]{2,1,0:T(8,128)S(1)} %get-tuple-element.22), channel_id=1, source_target_pairs={{0,1},{1,2},{2,3},{3,4},{4,5},{5,6},{6,7},{8,9},{9,10},{10,11},{11... | collective-permute-start | bytes 491528 | tf_op jit(solution)/shard_map/ppermute | solution.py:550
  12.7 5.5 %collective-permute-start.2 = (f32[216,128]{1,0:T(8,128)S(1)}, f32[216,128]{1,0:T(8,128)S(1)}, u32[]{:S(2)}, u32[]{:S(2)}) collective-permute-start(f32[216,128]{1,0:T(8,128)S(1)} %get-tuple-element.24.up), channel_id=1, source_target_pairs={{0,8},{8,16},{16,24},{24,32},{32,40},{40,48},{48,56},{1,9},{9,17},... | collective-permute-start | bytes 331784 | tf_op jit(solution)/shard_map/ppermute | solution.py:550
  15.8 7.6 %collective-permute-start.3 = (f32[216,128]{1,0:T(8,128)S(1)}, f32[216,128]{1,0:T(8,128)S(1)}, u32[]{:S(2)}, u32[]{:S(2)}) collective-permute-start(f32[216,128]{1,0:T(8,128)S(1)} %get-tuple-element.25.down), channel_id=1, source_target_pairs={{8,0},{16,8},{24,16},{32,24},{40,32},{48,40},{56,48},{9,1},{17,9},... | collective-permute-start | bytes 331784 | tf_op jit(solution)/shard_map/ppermute | solution.py:550
  23.8 9.7 %collective-permute-start.5 = (f32[8,8,128]{2,1,0:T(8,128)S(1)}, f32[8,8,128]{2,1,0:T(8,128)S(1)}, u32[]{:S(2)}, u32[]{:S(2)}) collective-permute-start(f32[8,8,128]{2,1,0:T(8,128)S(1)} %get-tuple-element.31.packed), channel_id=1, source_target_pairs={{64,128},{128,64},{192,256},{256,192},{320,384},{384,320},{448,0},... | collective-permute-start | bytes 98312 | tf_op jit(solution)/shard_map/ppermute | solution.py:550
  31.2 3.1 %collective-permute-start.4 = (f32[8,8,128]{2,1,0:T(8,128)S(1)}, f32[8,8,128]{2,1,0:T(8,128)S(1)}, u32[]{:S(2)}, u32[]{:S(2)}) collective-permute-start(f32[8,8,128]{2,1,0:T(8,128)S(1)} %get-tuple-element.31.packed), channel_id=1, source_target_pairs={{0,64},{64,0},{128,192},{192,128},{256,320},{320,256},{384,448},{4... | collective-permute-start | bytes 98312 | tf_op jit(solution)/shard_map/ppermute | solution.py:550

commit v5 on v4

--- a/solution.py
+++ b/solution.py
@@ -439,7 +439,7 @@
             ready[i, z] = part
 
 
-def adjoint_kernel(states, sense, ready, packed, one, two, por, kind, out_hbm, sense_hbm, out, sum_, sides, done):
+def adjoint_kernel(states, sense, ready, packed, one, two, por, kind, out, sense_out, sides):
     lane = lax.broadcasted_iota(jnp.int32, (NY, NX), 1)
     row = lax.broadcasted_iota(jnp.int32, (NY, NX), 0)
     before, after = from_side("gx", one, two)
@@ -484,7 +484,6 @@
             return jnp.where(first_two, turned, pltpu.roll(tile, 1, 1))
         return jnp.where(outer, pltpu.roll(sides[q], NX - 1 - 4 * t, 1), tile)
 
-    copies = []
     for z in range(NZ):
         h = []
         for q in range(Q):
@@ -503,15 +502,9 @@
             [ready[i, z] for i in range(STATE)], h, por[z], kind[z], range(Q)
         )
         for q in range(Q):
-            out[z, q] = back[q]
-        copies.append(pltpu.make_async_copy(out.at[z], out_hbm.at[:, z], done.at[z]))
-        copies[-1].start()
+            out[q, z] = back[q]
         then = jnp.where(outer, pltpu.roll(by_porosity, NX - 1 - 4 * (z + 1), 1), sense[z])
-        sum_[z] = then + now
-    copies.append(pltpu.make_async_copy(sum_, sense_hbm, done.at[NZ]))
-    copies[-1].start()
-    for copy in copies:
-        copy.wait()
+        sense_out[z] = then + now
 
 
 VMEM = pl.BlockSpec(memory_space=pltpu.VMEM)
@@ -592,13 +585,7 @@
         adjoint_kernel,
         [(Q, NZ, *tile), (NZ, *tile)],
         [VMEM] * 8,
-        [
-            pltpu.VMEM((NZ, Q, *tile), jnp.float32),
-            pltpu.VMEM((NZ, *tile), jnp.float32),
-            pltpu.VMEM((Q, *tile), jnp.float32),
-            pltpu.SemaphoreType.DMA((NZ + 1,)),
-        ],
-        out_specs=[HBM] * 2,
+        [pltpu.VMEM((Q, *tile), jnp.float32)],
     )(states, part, ready, packed, one, two, por, kind)
     return adjoint, sense
 

time: 35.8 us -> 35.8 us (level)
  no operation moved by 1% of the time
where the time goes in v5:
time: 35.8 us; the launch traced here: 35.5 us
  starting transfers between devices  19.9 us (56%)
  waiting for transfers between devices  11 us (31%)
  Pallas kernels  3.26 us (9%)
  between operations  1.36 us (4%)
    ppermute x6, starting transfers between devices, both_ways(): return (lax.ppermute(first, axis, one), lax.ppermute(second, axis, two))  19.9 us
    ppermute x6, waiting for transfers between devices, both_ways(): return (lax.ppermute(first, axis, one), lax.ppermute(second, axis, two))  11 us
    pallas_call x1, Pallas kernels, on_device(): call(adjoint_kernel, [(Q, NZ, *tile), (NZ, *tile)], [VMEM] * 8, [pltpu.VM...  1.26 us
    pallas_call x1, Pallas kernels, on_device(): call(collide_kernel, [(Q, NZ, *tile), (len(Z_UP), *tile), (len(Z_DOWN), *...  1.19 us
  transfers between devices with their start and end apart: 6, of which 5 were waited for; matrix products, arithmetic and copies ran while one was open for 0% of the time, Pallas kernels for 1%

profile of v5, /device:TPU:279, one launch (start us, length us, event | category | flops | bytes accessed | tf_op | source)
XLA Modules:
  0.0 35.5 jit_solution(2448384514151400997)
XLA Ops:
  1.3 1.2 %shard_map.68 = (f32[19,4,8,128]{3,2,1,0:T(8,128)S(1)}, f32[40,8,128]{2,1,0:T(8,128)S(1)}, f32[40,8,128]{2,1,0:T(8,128)S(1)}, f32[19,4,8,128]{3,2,1,0:T(8,128)S(...) custom-call(s32[1]{0:T(128)S(6)} %copy.7.step, f32[19,4,8,128]{3,2,1,0:T(8,128)} %pop_hbm.1, ...), custom_call_target="tpu_custom_call" | custom-call | tf_op jit(solution)/shard_map/pallas_call | solution.py:548
  2.5 1.9 %collective-permute-start = (f32[40,8,128]{2,1,0:T(8,128)S(1)}, f32[40,8,128]{2,1,0:T(8,128)S(1)}, u32[]{:S(2)}, u32[]{:S(2)}) collective-permute-start(f32[40,8,128]{2,1,0:T(8,128)S(1)} %get-tuple-element.21), channel_id=1, source_target_pairs={{1,0},{2,1},{3,2},{4,3},{5,4},{6,5},{7,6},{9,8},{10,9},{11,10},{12... | collective-permute-start | bytes 491528 | tf_op jit(solution)/shard_map/ppermute | solution.py:543
  4.4 3.4 %collective-permute-start.1 = (f32[40,8,128]{2,1,0:T(8,128)S(1)}, f32[40,8,128]{2,1,0:T(8,128)S(1)}, u32[]{:S(2)}, u32[]{:S(2)}) collective-permute-start(f32[40,8,128]{2,1,0:T(8,128)S(1)} %get-tuple-element.22), channel_id=1, source_target_pairs={{0,1},{1,2},{2,3},{3,4},{4,5},{5,6},{6,7},{8,9},{9,10},{10,11},{11... | collective-permute-start | bytes 491528 | tf_op jit(solution)/shard_map/ppermute | solution.py:543
  7.8 1.7 %collective-permute-done.refs_4_ = f32[40,8,128]{2,1,0:T(8,128)S(1)} collective-permute-done((f32[40,8,128]{2,1,0:T(8,128)S(1)}, f32[40,8,128]{2,1,0:T(8,128)S(1)}, u32[]{:S(2)}, u32[]{:S(2)}) %collective-permute-start) | collective-permute-done | bytes 163872 | tf_op jit(solution)/shard_map/ppermute | solution.py:543
  9.4 3.1 %collective-permute-done.1.refs_5_ = f32[40,8,128]{2,1,0:T(8,128)S(1)} collective-permute-done((f32[40,8,128]{2,1,0:T(8,128)S(1)}, f32[40,8,128]{2,1,0:T(8,128)S(1)}, u32[]{:S(2)}, u32[]{:S(2)}) %collective-permute-start.1) | collective-permute-done | bytes 163872 | tf_op jit(solution)/shard_map/ppermute | solution.py:543
  12.6 0.1 shard_map.69
  12.7 3.1 %collective-permute-start.2 = (f32[216,128]{1,0:T(8,128)S(1)}, f32[216,128]{1,0:T(8,128)S(1)}, u32[]{:S(2)}, u32[]{:S(2)}) collective-permute-start(f32[216,128]{1,0:T(8,128)S(1)} %get-tuple-element.24.up), channel_id=1, source_target_pairs={{0,8},{8,16},{16,24},{24,32},{32,40},{40,48},{48,56},{1,9},{9,17},... | collective-permute-start | bytes 331784 | tf_op jit(solution)/shard_map/ppermute | solution.py:543
  15.8 2.2 %collective-permute-start.3 = (f32[216,128]{1,0:T(8,128)S(1)}, f32[216,128]{1,0:T(8,128)S(1)}, u32[]{:S(2)}, u32[]{:S(2)}) collective-permute-start(f32[216,128]{1,0:T(8,128)S(1)} %get-tuple-element.25.down), channel_id=1, source_target_pairs={{8,0},{16,8},{24,16},{32,24},{40,32},{48,40},{56,48},{9,1},{17,9},... | collective-permute-start | bytes 331784 | tf_op jit(solution)/shard_map/ppermute | solution.py:543
  18.0 0.2 collective-permute-done.2.one
  18.2 5.2 %collective-permute-done.3.two = f32[216,128]{1,0:T(8,128)S(1)} collective-permute-done((f32[216,128]{1,0:T(8,128)S(1)}, f32[216,128]{1,0:T(8,128)S(1)}, u32[]{:S(2)}, u32[]{:S(2)}) %collective-permute-start.3) | collective-permute-done | bytes 110624 | tf_op jit(solution)/shard_map/ppermute | solution.py:543
  23.4 0.3 shard_map.70
  23.8 7.4 %collective-permute-start.5 = (f32[8,8,128]{2,1,0:T(8,128)S(1)}, f32[8,8,128]{2,1,0:T(8,128)S(1)}, u32[]{:S(2)}, u32[]{:S(2)}) collective-permute-start(f32[8,8,128]{2,1,0:T(8,128)S(1)} %get-tuple-element.31.packed), channel_id=1, source_target_pairs={{64,128},{128,64},{192,256},{256,192},{320,384},{384,320},{448,0},... | collective-permute-start | bytes 98312 | tf_op jit(solution)/shard_map/ppermute | solution.py:543
  31.2 1.9 %collective-permute-start.4 = (f32[8,8,128]{2,1,0:T(8,128)S(1)}, f32[8,8,128]{2,1,0:T(8,128)S(1)}, u32[]{:S(2)}, u32[]{:S(2)}) collective-permute-start(f32[8,8,128]{2,1,0:T(8,128)S(1)} %get-tuple-element.31.packed), channel_id=1, source_target_pairs={{0,64},{64,0},{128,192},{192,128},{256,320},{320,256},{384,448},{4... | collective-permute-start | bytes 98312 | tf_op jit(solution)/shard_map/ppermute | solution.py:543
  33.1 0.4 %shard_map.71 = (f32[1368,128]{1,0:T(8,128)S(1)}, f32[4,8,128]{2,1,0:T(8,128)S(1)}, f32[5,4,8,128]{3,2,1,0:T(8,128)S(1)}) custom-call(f32[1920,128]{1,0:T(8,128)S(1)} %get-tuple-element.26.wide, f32[19,4,8,128]{3,2,1,0:T(8,128)S(1)} %get-tuple-element.27.pop, f32[4,8,128]{2,1,0:T(8,128)S(1)} %get-tuple-element.19.refs_2_.por, ...), custom_call_target="tpu_custom_call" | custom-call | flops 20000000 | bytes 4000000 | tf_op jit(solution)/shard_map/pallas_call | solution.py:578
  33.5 0.0 collective-permute-done.5.two
  33.5 0.8 %collective-permute-done.4.one = f32[8,8,128]{2,1,0:T(8,128)S(1)} collective-permute-done((f32[8,8,128]{2,1,0:T(8,128)S(1)}, f32[8,8,128]{2,1,0:T(8,128)S(1)}, u32[]{:S(2)}, u32[]{:S(2)}) %collective-permute-start.4) | collective-permute-done | bytes 32800 | tf_op jit(solution)/shard_map/ppermute | solution.py:543
  34.3 1.3 %shard_map.72 = (f32[19,4,8,128]{3,2,1,0:T(8,128)}, f32[4,8,128]{2,1,0:T(8,128)}) custom-call(f32[1368,128]{1,0:T(8,128)S(1)} %get-tuple-element.28.states, f32[4,8,128]{2,1,0:T(8,128)S(1)} %get-tuple-element.29.sense, f32[5,4,8,128]{3,2,1,0:T(8,128)S(1)} %get-tuple-element.30.ready, f32[8,8,128]{2,1,0:T(8,128)S(1)} %get-tuple-element.31.packed, ...), custom_call_target="tpu_custom_call" | custom-call | tf_op jit(solution)/shard_map/pallas_call | solution.py:584
Async XLA Ops:
  2.5 7.0 %collective-permute-start = (f32[40,8,128]{2,1,0:T(8,128)S(1)}, f32[40,8,128]{2,1,0:T(8,128)S(1)}, u32[]{:S(2)}, u32[]{:S(2)}) collective-permute-start(f32[40,8,128]{2,1,0:T(8,128)S(1)} %get-tuple-element.21), channel_id=1, source_target_pairs={{1,0},{2,1},{3,2},{4,3},{5,4},{6,5},{7,6},{9,8},{10,9},{11,10},{12... | collective-permute-start | bytes 491528 | tf_op jit(solution)/shard_map/ppermute | solution.py:543
  4.4 8.2 %collective-permute-start.1 = (f32[40,8,128]{2,1,0:T(8,128)S(1)}, f32[40,8,128]{2,1,0:T(8,128)S(1)}, u32[]{:S(2)}, u32[]{:S(2)}) collective-permute-start(f32[40,8,128]{2,1,0:T(8,128)S(1)} %get-tuple-element.22), channel_id=1, source_target_pairs={{0,1},{1,2},{2,3},{3,4},{4,5},{5,6},{6,7},{8,9},{9,10},{10,11},{11... | collective-permute-start | bytes 491528 | tf_op jit(solution)/shard_map/ppermute | solution.py:543
  12.7 5.5 %collective-permute-start.2 = (f32[216,128]{1,0:T(8,128)S(1)}, f32[216,128]{1,0:T(8,128)S(1)}, u32[]{:S(2)}, u32[]{:S(2)}) collective-permute-start(f32[216,128]{1,0:T(8,128)S(1)} %get-tuple-element.24.up), channel_id=1, source_target_pairs={{0,8},{8,16},{16,24},{24,32},{32,40},{40,48},{48,56},{1,9},{9,17},... | collective-permute-start | bytes 331784 | tf_op jit(solution)/shard_map/ppermute | solution.py:543
  15.8 7.6 %collective-permute-start.3 = (f32[216,128]{1,0:T(8,128)S(1)}, f32[216,128]{1,0:T(8,128)S(1)}, u32[]{:S(2)}, u32[]{:S(2)}) collective-permute-start(f32[216,128]{1,0:T(8,128)S(1)} %get-tuple-element.25.down), channel_id=1, source_target_pairs={{8,0},{16,8},{24,16},{32,24},{40,32},{48,40},{56,48},{9,1},{17,9},... | collective-permute-start | bytes 331784 | tf_op jit(solution)/shard_map/ppermute | solution.py:543
  23.8 9.7 %collective-permute-start.5 = (f32[8,8,128]{2,1,0:T(8,128)S(1)}, f32[8,8,128]{2,1,0:T(8,128)S(1)}, u32[]{:S(2)}, u32[]{:S(2)}) collective-permute-start(f32[8,8,128]{2,1,0:T(8,128)S(1)} %get-tuple-element.31.packed), channel_id=1, source_target_pairs={{64,128},{128,64},{192,256},{256,192},{320,384},{384,320},{448,0},... | collective-permute-start | bytes 98312 | tf_op jit(solution)/shard_map/ppermute | solution.py:543
  31.2 3.1 %collective-permute-start.4 = (f32[8,8,128]{2,1,0:T(8,128)S(1)}, f32[8,8,128]{2,1,0:T(8,128)S(1)}, u32[]{:S(2)}, u32[]{:S(2)}) collective-permute-start(f32[8,8,128]{2,1,0:T(8,128)S(1)} %get-tuple-element.31.packed), channel_id=1, source_target_pairs={{0,64},{64,0},{128,192},{192,128},{256,320},{320,256},{384,448},{4... | collective-permute-start | bytes 98312 | tf_op jit(solution)/shard_map/ppermute | solution.py:543

commit v6 on v5

--- a/solution.py
+++ b/solution.py
@@ -332,7 +332,7 @@
         by_side("gy", functools.partial(copy_both, up, down), first, second)
 
 
-def columns_kernel(shifted, up, down, one, two, wide, packed):
+def columns_kernel(shifted, up, down, one, two, wide, packed, first, second):
     left, right = from_side("gy", one, two)
     row = lax.broadcasted_iota(jnp.int32, (NY, NX), 0)
     lane = lax.broadcasted_iota(jnp.int32, (NY, NX), 1)
@@ -389,6 +389,15 @@
                 total = turned if total is None else jnp.where(lane >= 4 * k, turned, total)
         packed[u] = total
 
+    def write(forward, backward):
+        low = (lane & 3) < 2
+        for v in range(PACKED // 2):
+            one_, two_ = packed[2 * v], packed[2 * v + 1]
+            forward[v] = jnp.where(low, one_, pltpu.roll(two_, 2, 1))
+            backward[v] = jnp.where(low, pltpu.roll(one_, NX - 2, 1), two_)
+
+    by_side("gx", write, first, second)
+
 
 STATE = 5
 
@@ -442,7 +451,14 @@
 def adjoint_kernel(states, sense, ready, packed, one, two, por, kind, out, sense_out, sides):
     lane = lax.broadcasted_iota(jnp.int32, (NY, NX), 1)
     row = lax.broadcasted_iota(jnp.int32, (NY, NX), 0)
-    before, after = from_side("gx", one, two)
+    low_half, high_half = from_side("gx", one, two)
+
+    def before(u):
+        return pltpu.roll(low_half(u // 2), NX - 2, 1) if u % 2 else low_half(u // 2)
+
+    def after(u):
+        return high_half(u // 2) if u % 2 else pltpu.roll(high_half(u // 2), 2, 1)
+
     slot = lane & 3
     ends = []
     for u in range(PACKED):
@@ -569,12 +585,12 @@
     if "gy" in REVERSED and not copies:
         first, second = down, up
     one, two = both_ways(first, second, "gy")
-    wide, packed = call(
+    wide, packed, first, second = call(
         columns_kernel,
-        [(len(X_FIELDS) * (EXT + 2) * ROWS, NX), (PACKED, *tile)],
+        [(len(X_FIELDS) * (EXT + 2) * ROWS, NX), (PACKED, *tile)] + [(PACKED // 2, *tile)] * 2,
         [VMEM] * 5,
     )(shifted, up, down, one, two)
-    one, two = both_ways(packed, packed, "gx")
+    one, two = both_ways(first, second, "gx")
     states, part, ready = call(
         inner_kernel,
         [(Q * (SIDES + 1) * ROWS, NX), (NZ, *tile), (STATE, NZ, *tile)],

time: 35.8 us -> 37.5 us (1.047)
  waiting for transfers between devices: 11 us -> 12.6 us
    ppermute x6, waiting for transfers between devices: 11 us -> 12.6 us  [both_ways(): return (lax.ppermute(first, axis, one), lax.ppermute(second, axis, two))]
where the time goes in v6:
time: 37.5 us; the launch traced here: 37.2 us
  starting transfers between devices  19.9 us (53%)
  waiting for transfers between devices  12.6 us (34%)
  Pallas kernels  3.41 us (9%)
  between operations  1.35 us (4%)
    ppermute x6, starting transfers between devices, both_ways(): return (lax.ppermute(first, axis, one), lax.ppermute(second, axis, two))  19.9 us
    ppermute x6, waiting for transfers between devices, both_ways(): return (lax.ppermute(first, axis, one), lax.ppermute(second, axis, two))  12.6 us
    pallas_call x1, Pallas kernels, on_device(): call(adjoint_kernel, [(Q, NZ, *tile), (NZ, *tile)], [VMEM] * 8, [pltpu.VM...  1.33 us
    pallas_call x1, Pallas kernels, on_device(): call(collide_kernel, [(Q, NZ, *tile), (len(Z_UP), *tile), (len(Z_DOWN), *...  1.19 us
  transfers between devices with their start and end apart: 6, of which 5 were waited for; matrix products, arithmetic and copies ran while one was open for 0% of the time, Pallas kernels for 1%

profile of v6, /device:TPU:279, one launch (start us, length us, event | category | flops | bytes accessed | tf_op | source)
XLA Modules:
  0.0 37.2 jit_solution(15994376889334918791)
XLA Ops:
  1.3 1.2 %shard_map.68 = (f32[19,4,8,128]{3,2,1,0:T(8,128)S(1)}, f32[40,8,128]{2,1,0:T(8,128)S(1)}, f32[40,8,128]{2,1,0:T(8,128)S(1)}, f32[19,4,8,128]{3,2,1,0:T(8,128)S(...) custom-call(s32[1]{0:T(128)S(6)} %copy.7.step, f32[19,4,8,128]{3,2,1,0:T(8,128)} %pop_hbm.1, ...), custom_call_target="tpu_custom_call" | custom-call | tf_op jit(solution)/shard_map/pallas_call | solution.py:564
  2.5 1.9 %collective-permute-start = (f32[40,8,128]{2,1,0:T(8,128)S(1)}, f32[40,8,128]{2,1,0:T(8,128)S(1)}, u32[]{:S(2)}, u32[]{:S(2)}) collective-permute-start(f32[40,8,128]{2,1,0:T(8,128)S(1)} %get-tuple-element.23), channel_id=1, source_target_pairs={{1,0},{2,1},{3,2},{4,3},{5,4},{6,5},{7,6},{9,8},{10,9},{11,10},{12... | collective-permute-start | bytes 491528 | tf_op jit(solution)/shard_map/ppermute | solution.py:559
  4.4 3.4 %collective-permute-start.1 = (f32[40,8,128]{2,1,0:T(8,128)S(1)}, f32[40,8,128]{2,1,0:T(8,128)S(1)}, u32[]{:S(2)}, u32[]{:S(2)}) collective-permute-start(f32[40,8,128]{2,1,0:T(8,128)S(1)} %get-tuple-element.24), channel_id=1, source_target_pairs={{0,1},{1,2},{2,3},{3,4},{4,5},{5,6},{6,7},{8,9},{9,10},{10,11},{11... | collective-permute-start | bytes 491528 | tf_op jit(solution)/shard_map/ppermute | solution.py:559
  7.8 1.7 %collective-permute-done.refs_4_ = f32[40,8,128]{2,1,0:T(8,128)S(1)} collective-permute-done((f32[40,8,128]{2,1,0:T(8,128)S(1)}, f32[40,8,128]{2,1,0:T(8,128)S(1)}, u32[]{:S(2)}, u32[]{:S(2)}) %collective-permute-start) | collective-permute-done | bytes 163872 | tf_op jit(solution)/shard_map/ppermute | solution.py:559
  9.4 3.1 %collective-permute-done.1.refs_5_ = f32[40,8,128]{2,1,0:T(8,128)S(1)} collective-permute-done((f32[40,8,128]{2,1,0:T(8,128)S(1)}, f32[40,8,128]{2,1,0:T(8,128)S(1)}, u32[]{:S(2)}, u32[]{:S(2)}) %collective-permute-start.1) | collective-permute-done | bytes 163872 | tf_op jit(solution)/shard_map/ppermute | solution.py:559
  12.6 0.1 shard_map.69
  12.7 3.1 %collective-permute-start.2 = (f32[216,128]{1,0:T(8,128)S(1)}, f32[216,128]{1,0:T(8,128)S(1)}, u32[]{:S(2)}, u32[]{:S(2)}) collective-permute-start(f32[216,128]{1,0:T(8,128)S(1)} %get-tuple-element.26.up), channel_id=1, source_target_pairs={{0,8},{8,16},{16,24},{24,32},{32,40},{40,48},{48,56},{1,9},{9,17},... | collective-permute-start | bytes 331784 | tf_op jit(solution)/shard_map/ppermute | solution.py:559
  15.8 2.2 %collective-permute-start.3 = (f32[216,128]{1,0:T(8,128)S(1)}, f32[216,128]{1,0:T(8,128)S(1)}, u32[]{:S(2)}, u32[]{:S(2)}) collective-permute-start(f32[216,128]{1,0:T(8,128)S(1)} %get-tuple-element.27.down), channel_id=1, source_target_pairs={{8,0},{16,8},{24,16},{32,24},{40,32},{48,40},{56,48},{9,1},{17,9},... | collective-permute-start | bytes 331784 | tf_op jit(solution)/shard_map/ppermute | solution.py:559
  18.0 0.2 collective-permute-done.2.one
  18.2 5.2 %collective-permute-done.3.two = f32[216,128]{1,0:T(8,128)S(1)} collective-permute-done((f32[216,128]{1,0:T(8,128)S(1)}, f32[216,128]{1,0:T(8,128)S(1)}, u32[]{:S(2)}, u32[]{:S(2)}) %collective-permute-start.3) | collective-permute-done | bytes 110624 | tf_op jit(solution)/shard_map/ppermute | solution.py:559
  23.4 0.4 %shard_map.70 = (f32[1920,128]{1,0:T(8,128)S(1)}, f32[8,8,128]{2,1,0:T(8,128)S(1)}, f32[4,8,128]{2,1,0:T(8,128)S(1)}, f32[4,8,128]{2,1,0:T(8,128)S(1)}) custom-call(f32[1680,128]{1,0:T(8,128)S(1)} %get-tuple-element.25.shifted, f32[216,128]{1,0:T(8,128)S(1)} %get-tuple-element.26.up, f32[216,128]{1,0:T(8,128)S(1)} %get-tuple-element.27.down, ...), custom_call_target="tpu_custom_call" | custom-call | tf_op jit(solution)/shard_map/pallas_call | solution.py:588
  23.8 4.9 %collective-permute-start.4 = (f32[4,8,128]{2,1,0:T(8,128)S(1)}, f32[4,8,128]{2,1,0:T(8,128)S(1)}, u32[]{:S(2)}, u32[]{:S(2)}) collective-permute-start(f32[4,8,128]{2,1,0:T(8,128)S(1)} %get-tuple-element.34), channel_id=1, source_target_pairs={{0,64},{64,0},{128,192},{192,128},{256,320},{320,256},{384,448},{4... | collective-permute-start | bytes 49160 | tf_op jit(solution)/shard_map/ppermute | solution.py:559
  28.7 4.4 %collective-permute-start.5 = (f32[4,8,128]{2,1,0:T(8,128)S(1)}, f32[4,8,128]{2,1,0:T(8,128)S(1)}, u32[]{:S(2)}, u32[]{:S(2)}) collective-permute-start(f32[4,8,128]{2,1,0:T(8,128)S(1)} %get-tuple-element.35), channel_id=1, source_target_pairs={{64,128},{128,64},{192,256},{256,192},{320,384},{384,320},{448,0},... | collective-permute-start | bytes 49160 | tf_op jit(solution)/shard_map/ppermute | solution.py:559
  33.2 0.4 shard_map.71
  33.5 0.0 collective-permute-done.4.one
  33.5 2.4 %collective-permute-done.5.two = f32[4,8,128]{2,1,0:T(8,128)S(1)} collective-permute-done((f32[4,8,128]{2,1,0:T(8,128)S(1)}, f32[4,8,128]{2,1,0:T(8,128)S(1)}, u32[]{:S(2)}, u32[]{:S(2)}) %collective-permute-start.5) | collective-permute-done | bytes 16416 | tf_op jit(solution)/shard_map/ppermute | solution.py:559
  35.9 1.3 %shard_map.72 = (f32[19,4,8,128]{3,2,1,0:T(8,128)}, f32[4,8,128]{2,1,0:T(8,128)}) custom-call(f32[1368,128]{1,0:T(8,128)S(1)} %get-tuple-element.30.states, f32[4,8,128]{2,1,0:T(8,128)S(1)} %get-tuple-element.31.sense, f32[5,4,8,128]{3,2,1,0:T(8,128)S(1)} %get-tuple-element.32.ready, f32[8,8,128]{2,1,0:T(8,128)S(1)} %get-tuple-element.33.packed, ...), custom_call_target="tpu_custom_call" | custom-call | tf_op jit(solution)/shard_map/pallas_call | solution.py:600
Async XLA Ops:
  2.5 7.0 %collective-permute-start = (f32[40,8,128]{2,1,0:T(8,128)S(1)}, f32[40,8,128]{2,1,0:T(8,128)S(1)}, u32[]{:S(2)}, u32[]{:S(2)}) collective-permute-start(f32[40,8,128]{2,1,0:T(8,128)S(1)} %get-tuple-element.23), channel_id=1, source_target_pairs={{1,0},{2,1},{3,2},{4,3},{5,4},{6,5},{7,6},{9,8},{10,9},{11,10},{12... | collective-permute-start | bytes 491528 | tf_op jit(solution)/shard_map/ppermute | solution.py:559
  4.4 8.2 %collective-permute-start.1 = (f32[40,8,128]{2,1,0:T(8,128)S(1)}, f32[40,8,128]{2,1,0:T(8,128)S(1)}, u32[]{:S(2)}, u32[]{:S(2)}) collective-permute-start(f32[40,8,128]{2,1,0:T(8,128)S(1)} %get-tuple-element.24), channel_id=1, source_target_pairs={{0,1},{1,2},{2,3},{3,4},{4,5},{5,6},{6,7},{8,9},{9,10},{10,11},{11... | collective-permute-start | bytes 491528 | tf_op jit(solution)/shard_map/ppermute | solution.py:559
  12.7 5.5 %collective-permute-start.2 = (f32[216,128]{1,0:T(8,128)S(1)}, f32[216,128]{1,0:T(8,128)S(1)}, u32[]{:S(2)}, u32[]{:S(2)}) collective-permute-start(f32[216,128]{1,0:T(8,128)S(1)} %get-tuple-element.26.up), channel_id=1, source_target_pairs={{0,8},{8,16},{16,24},{24,32},{32,40},{40,48},{48,56},{1,9},{9,17},... | collective-permute-start | bytes 331784 | tf_op jit(solution)/shard_map/ppermute | solution.py:559
  15.8 7.6 %collective-permute-start.3 = (f32[216,128]{1,0:T(8,128)S(1)}, f32[216,128]{1,0:T(8,128)S(1)}, u32[]{:S(2)}, u32[]{:S(2)}) collective-permute-start(f32[216,128]{1,0:T(8,128)S(1)} %get-tuple-element.27.down), channel_id=1, source_target_pairs={{8,0},{16,8},{24,16},{32,24},{40,32},{48,40},{56,48},{9,1},{17,9},... | collective-permute-start | bytes 331784 | tf_op jit(solution)/shard_map/ppermute | solution.py:559
  23.8 9.7 %collective-permute-start.4 = (f32[4,8,128]{2,1,0:T(8,128)S(1)}, f32[4,8,128]{2,1,0:T(8,128)S(1)}, u32[]{:S(2)}, u32[]{:S(2)}) collective-permute-start(f32[4,8,128]{2,1,0:T(8,128)S(1)} %get-tuple-element.34), channel_id=1, source_target_pairs={{0,64},{64,0},{128,192},{192,128},{256,320},{320,256},{384,448},{4... | collective-permute-start | bytes 49160 | tf_op jit(solution)/shard_map/ppermute | solution.py:559
  28.7 7.2 %collective-permute-start.5 = (f32[4,8,128]{2,1,0:T(8,128)S(1)}, f32[4,8,128]{2,1,0:T(8,128)S(1)}, u32[]{:S(2)}, u32[]{:S(2)}) collective-permute-start(f32[4,8,128]{2,1,0:T(8,128)S(1)} %get-tuple-element.35), channel_id=1, source_target_pairs={{64,128},{128,64},{192,256},{256,192},{320,384},{384,320},{448,0},... | collective-permute-start | bytes 49160 | tf_op jit(solution)/shard_map/ppermute | solution.py:559
